TPU v7x, 32 devices: a whole 2x2x4 slice. The times are simulated.
32 devices in a mesh: seq: 16 (over z, x, core), chan: 2 (over y).
Axes of the slice: x: 2, y: 2, z: 4, core: 2. Of those that a mesh axis runs over, the one named last changes fastest.
Arguments:
- query_in: bfloat16 [8192, 4096], P('seq', 'chan'), may hold values from -6 to 6
- key_in: bfloat16 [8192, 4096], P('seq', 'chan'), may hold values from -6 to 6
- value_in: bfloat16 [8192, 4096], P('seq', 'chan'), may hold values from -6 to 6
- short_weight: float32 [3, 3, 4096], P(None, None, 'chan'), may hold values from -3.5 to 3.5
- long_filter: float32 [256, 8192], P('chan', 'seq'), may hold values from 0 to 0.5
- skip_gain: float32 [4096], P('chan'), may hold values from 0.5 to 1.5
- w_out: bfloat16 [4096, 8192], P('chan', 'seq'), may hold values from -0.125 to 0.125
Outputs:
- mixer_out: bfloat16 [8192, 8192], P('seq', 'chan')
All inputs are finite; a program needn't handle non-finite values.
Results may differ from a plain program's by a relative error of at most 0.018.
Values may be sent and summed in bfloat16 or wider, within the bound.
A program may use at most 192 MiB of HBM per device.

v0:
```python
import math

import jax
import jax.numpy as jnp
from jax import lax
from jax.sharding import PartitionSpec as P

GROUP = 16
KW = 3


HIGHEST = lax.Precision.HIGHEST


def as_sent(value):
    return jax.tree.map(lambda a: a.astype(jnp.bfloat16) if a.dtype == jnp.float32 else a, value)


def passed_along(value, axis, by):
    devices = lax.axis_size(axis)
    pairs = [(i, i + by) for i in range(devices) if 0 <= i + by < devices]
    return lax.ppermute(value, axis, pairs)


def angles(rows, cols, period):
    row_ids = lax.broadcasted_iota(jnp.int32, (rows, cols), 0)
    col_ids = lax.broadcasted_iota(jnp.int32, (rows, cols), 1)
    phase = (row_ids * col_ids % period).astype(jnp.float32) * (2.0 * math.pi / period)
    return (jnp.cos(phase), jnp.sin(phase))


def twiddle(parts, piece_len, offset, total_len):
    freq = lax.broadcasted_iota(jnp.int32, (2 * parts, piece_len), 0)
    place = lax.broadcasted_iota(jnp.int32, (2 * parts, piece_len), 1) + offset
    phase = (freq * place % total_len).astype(jnp.float32) * (2.0 * math.pi / total_len)
    return (jnp.cos(phase), jnp.sin(phase))


def apply_table(form, table, data):
    return jnp.einsum(form, table, data, precision=HIGHEST)


def spread_forward(signal, parts, index):
    piece_len = signal.shape[1]
    total_len = 2 * parts * parts * piece_len
    cos_one, sin_one = angles(2 * parts, parts, 2 * parts)
    first_re = apply_table("kn,nsx->ksx", cos_one, signal)
    first_im = -apply_table("kn,nsx->ksx", sin_one, signal)
    tw_cos, tw_sin = twiddle(parts, piece_len, index * piece_len, total_len)
    tw_cos = tw_cos[:, :, None]
    tw_sin = tw_sin[:, :, None]
    return (first_re * tw_cos + first_im * tw_sin, first_im * tw_cos - first_re * tw_sin)


def spread_second(real_part, imag_part):
    length = real_part.shape[1]
    cos_two, sin_two = angles(length, length, length)
    out_re = apply_table("kn,anx->akx", cos_two, real_part) + apply_table(
        "kn,anx->akx", sin_two, imag_part
    )
    out_im = apply_table("kn,anx->akx", cos_two, imag_part) - apply_table(
        "kn,anx->akx", sin_two, real_part
    )
    return (out_re, out_im)


def spread_back_second(real_part, imag_part):
    length = real_part.shape[1]
    cos_two, sin_two = angles(length, length, length)
    out_re = apply_table("nk,akx->anx", cos_two, real_part) - apply_table(
        "nk,akx->anx", sin_two, imag_part
    )
    out_im = apply_table("nk,akx->anx", cos_two, imag_part) + apply_table(
        "nk,akx->anx", sin_two, real_part
    )
    return (out_re, out_im)


def spread_back_first(real_part, imag_part, parts, index):
    piece_len = real_part.shape[1]
    total_len = 2 * parts * parts * piece_len
    tw_cos, tw_sin = twiddle(parts, piece_len, index * piece_len, total_len)
    tw_cos = tw_cos[:, :, None]
    tw_sin = tw_sin[:, :, None]
    turned_re = real_part * tw_cos - imag_part * tw_sin
    turned_im = imag_part * tw_cos + real_part * tw_sin
    cos_one, sin_one = angles(2 * parts, parts, 2 * parts)
    summed = apply_table("kn,ksx->nsx", cos_one, turned_re) - apply_table(
        "kn,ksx->nsx", sin_one, turned_im
    )
    return summed * (1.0 / total_len)


def spread_conv(gated, long_filter, parts, index):
    signal = lax.all_to_all(gated[None], "seq", split_axis=1, concat_axis=0, tiled=True).astype(
        jnp.float32
    )
    filt_rows = lax.all_to_all(
        jnp.transpose(long_filter)[None].astype(jnp.bfloat16),
        "seq",
        split_axis=1,
        concat_axis=0,
        tiled=True,
    ).astype(jnp.float32)
    data_re, data_im = spread_forward(signal, parts, index)
    filt_re, filt_im = spread_forward(filt_rows, parts, index)
    data_re, data_im, filt_re, filt_im = (
        lax.all_to_all(
            data_re.astype(jnp.bfloat16), "seq", split_axis=0, concat_axis=1, tiled=True
        ).astype(data_re.dtype),
        lax.all_to_all(
            data_im.astype(jnp.bfloat16), "seq", split_axis=0, concat_axis=1, tiled=True
        ).astype(data_im.dtype),
        lax.all_to_all(as_sent(filt_re), "seq", split_axis=0, concat_axis=1, tiled=True).astype(
            filt_re.dtype
        ),
        lax.all_to_all(as_sent(filt_im), "seq", split_axis=0, concat_axis=1, tiled=True).astype(
            filt_im.dtype
        ),
    )
    data_re, data_im = spread_second(data_re, data_im)
    filt_re, filt_im = spread_second(filt_re, filt_im)
    filt_re = jnp.repeat(filt_re, GROUP, axis=2)
    filt_im = jnp.repeat(filt_im, GROUP, axis=2)
    prod_re = data_re * filt_re - data_im * filt_im
    prod_im = data_re * filt_im + data_im * filt_re
    back_re, back_im = spread_back_second(prod_re, prod_im)
    back_re, back_im = (
        lax.all_to_all(as_sent(back_re), "seq", split_axis=1, concat_axis=0, tiled=True).astype(
            back_re.dtype
        ),
        lax.all_to_all(as_sent(back_im), "seq", split_axis=1, concat_axis=0, tiled=True).astype(
            back_im.dtype
        ),
    )
    result = spread_back_first(back_re, back_im, parts, index).astype(jnp.bfloat16)
    return lax.all_to_all(result, "seq", split_axis=0, concat_axis=1, tiled=True)[0]


def on_device(query_in, key_in, value_in, short_weight, long_filter, skip_gain, w_out):
    local_len, width = query_in.shape
    parts = lax.axis_size("seq")
    index = lax.axis_index("seq")
    stacked = jnp.stack([query_in, key_in, value_in])
    border = passed_along(stacked[:, local_len - (KW - 1) :, :], "seq", 1)
    extended = jnp.concatenate([border, stacked], axis=1)
    convolved = short_weight[:, 0, None, :] * extended[:, KW - 1 : KW - 1 + local_len, :].astype(
        jnp.float32
    )
    for shift in range(1, KW):
        convolved = convolved + short_weight[:, shift, None, :] * extended[
            :, KW - 1 - shift : KW - 1 - shift + local_len, :
        ].astype(jnp.float32)
    query_conv = convolved[0].astype(jnp.bfloat16)
    gated = (convolved[1] * convolved[2]).astype(jnp.bfloat16)
    conv = spread_conv(gated, long_filter, parts, index)
    mixed = (
        query_conv.astype(jnp.float32)
        * (conv.astype(jnp.float32) + skip_gain * gated.astype(jnp.float32))
    ).astype(jnp.bfloat16)
    terms = jnp.dot(
        mixed, lax.all_gather(w_out, "seq", axis=1, tiled=True), preferred_element_type=jnp.float32
    )
    return lax.psum_scatter(terms.astype(jnp.bfloat16), "chan", scatter_dimension=1, tiled=True)


def solution(mesh):
    placed = (
        P("seq", "chan"),
        P("seq", "chan"),
        P("seq", "chan"),
        P(None, None, "chan"),
        P("chan", "seq"),
        P("chan"),
        P("chan", "seq"),
    )
    return jax.shard_map(
        on_device, mesh=mesh, in_specs=placed, out_specs=P("seq", "chan"), check_vma=False
    )
```

profile of v0, /device:TPU:0, one launch (start us, length us, event | category | flops | bytes accessed | tf_op | source)
XLA Modules:
  0.0 972.2 jit_solution(5754068755744894752)
XLA Ops:
  43.5 13.1 %reduce = bf16[512,2048]{1,0:T(8,128)(2,1)S(1)} reduce(bf16[512,1,2048]{2,1,0:T(2,128)(2,1)} %bitcast.171, bf16[]{:T(256)} %broadcast.245), dimensions={1}, to_apply=%bitcast.152.reduce_sub_computation | reduce | bytes 4194306
  67.8 71.3 %all-to-all-done = bf16[16,2,32768]{2,1,0:T(2,128)(2,1)S(1)} async-done(((bf16[16,2,32768]{2,1,0:T(2,128)(2,1)}), bf16[16,2,32768]{2,1,0:T(2,128)(2,1)S(1)}, u32[]{:S(2)}, u32[]{:S(2)}) %all-to-all-start) | async-done | bytes 2097184 | tf_op jit(solution)/shard_map/all_to_all | solution.py:95
  192.5 99.7 %all-to-all-done.1 = bf16[32,32,2048]{2,1,0:T(8,128)(2,1)} async-done(((bf16[32,32,2048]{2,1,0:T(8,128)(2,1)}), bf16[32,32,2048]{2,1,0:T(8,128)(2,1)}, u32[]{:S(2)}, u32[]{:S(2)}) %all-to-all-start.1) | async-done | bytes 4194336 | tf_op jit(solution)/shard_map/all_to_all | solution.py:108
  292.2 36.7 %all-to-all-start.2 = ((bf16[32,32,2048]{2,1,0:T(8,128)(2,1)}), bf16[32,32,2048]{2,1,0:T(8,128)(2,1)}, u32[]{:S(2)}, u32[]{:S(2)}) async-start(bf16[32,32,2048]{2,1,0:T(8,128)(2,1)} %copy.67), calls=%async_computation.2 | async-start | bytes 8388608 | tf_op jit(solution)/shard_map/all_to_all | solution.py:111
  354.7 51.9 %all-to-all-done.2 = bf16[32,32,2048]{2,1,0:T(8,128)(2,1)} async-done(((bf16[32,32,2048]{2,1,0:T(8,128)(2,1)}), bf16[32,32,2048]{2,1,0:T(8,128)(2,1)}, u32[]{:S(2)}, u32[]{:S(2)}) %all-to-all-start.2) | async-done | bytes 4194336 | tf_op jit(solution)/shard_map/all_to_all | solution.py:111
  410.0 12.3 %fusion.52 = f32[2,2048,512]{2,1,0:T(8,128)S(1)} fusion(bf16[2,512,2048]{2,1,0:T(8,128)(2,1)S(1)} %bitcast.154), kind=kOutput, calls=%fused_computation.74 | convolution fusion | flops 12888571904 | bytes 12582912 | tf_op jit(solution)/shard_map/kn,anx->akx/dot_general | solution.py:40
  422.3 15.1 %fusion.48 = f32[2,2048,512]{2,1,0:T(8,128)} fusion(bf16[2,512,2048]{2,1,0:T(8,128)(2,1)S(1)} %bitcast.156), kind=kOutput, calls=%fused_computation.70 | convolution fusion | flops 12888571904 | bytes 12582912 | tf_op jit(solution)/shard_map/kn,anx->akx/dot_general | solution.py:40
  437.4 15.8 %convolution_add_fusion = f32[2,2048,512]{2,1,0:T(8,128)} fusion(f32[2,2048,512]{2,1,0:T(8,128)S(1)} %fusion.52, bf16[2,512,2048]{2,1,0:T(8,128)(2,1)S(1)} %bitcast.157), kind=kOutput, calls=%fused_computation.39 | convolution fusion | flops 12890669056 | bytes 20971520 | tf_op jit(solution)/shard_map/kn,anx->akx/dot_general | solution.py:40
  453.3 22.5 %fusion.1 = (f32[2,512,2048]{1,2,0:T(8,128)}, f32[2,512,2048]{1,2,0:T(8,128)}) fusion(f32[2,2048,512]{2,1,0:T(8,128)} %convolution_add_fusion, f32[2,512,128]{1,2,0:T(8,128)S(1)} %fusion.31, f32[2,512,128]{1,2,0:T(8,128)} %fusion.32, f32[2,2048,512]{2,1,0:T(8,128)} %fusion.48, bf16[2,512,2048]{2,1,0:T(8,128)(2,1)S(1)} %bitcast.155), kind=kOutput, calls=%fused_computation.7 | convolution fusion | flops 12903251968 | bytes 38797312 | tf_op jit(solution)/shard_map/kn,anx->akx/dot_general | solution.py:40
  475.8 23.8 %fusion.42 = f32[2,2048,512]{2,1,0:T(8,128)S(1)} fusion(f32[2,512,2048]{1,2,0:T(8,128)} %get-tuple-element.5), kind=kOutput, calls=%fused_computation.64 | convolution fusion | flops 12888571904 | bytes 16777216 | tf_op jit(solution)/shard_map/nk,akx->anx/dot_general | solution.py:40
  499.5 22.9 %fusion.11 = bf16[2,512,2048]{1,2,0:T(8,128)(2,1)} fusion(f32[2,2048,512]{2,1,0:T(8,128)S(1)} %fusion.42, f32[2,512,2048]{1,2,0:T(8,128)S(1)} %copy-done), kind=kOutput, calls=%fused_computation.25 | convolution fusion | flops 12892766208 | bytes 20971520 | tf_op jit(solution)/shard_map/nk,akx->anx/dot_general | solution.py:40
  522.4 11.3 %copy.87 = bf16[2,512,2048]{2,0,1:T(2,128)(2,1)} copy(bf16[2,512,2048]{1,2,0:T(8,128)(2,1)} %fusion.11) | data formatting | bytes 8388608 | tf_op jit(solution)/shard_map/convert_element_type | solution.py:16
  533.7 20.2 %all-to-all-start.7 = ((bf16[2,512,2048]{2,0,1:T(2,128)(2,1)}), bf16[2,512,2048]{2,0,1:T(2,128)(2,1)}, u32[]{:S(2)}, u32[]{:S(2)}) async-start(bf16[2,512,2048]{2,0,1:T(2,128)(2,1)} %copy.87), calls=%async_computation.7 | async-start | bytes 8388608 | tf_op jit(solution)/shard_map/all_to_all | solution.py:132
  553.9 23.5 %fusion.44 = f32[2,2048,512]{2,1,0:T(8,128)S(1)} fusion(f32[2,512,2048]{1,2,0:T(8,128)} %get-tuple-element.6), kind=kOutput, calls=%fused_computation.66 | convolution fusion | flops 12888571904 | bytes 16777216 | tf_op jit(solution)/shard_map/nk,akx->anx/dot_general | solution.py:40
  577.4 25.0 %fusion.10 = bf16[2,512,2048]{1,2,0:T(8,128)(2,1)} fusion(f32[2,2048,512]{2,1,0:T(8,128)S(1)} %fusion.44, f32[2,512,2048]{1,2,0:T(8,128)} %get-tuple-element.5), kind=kOutput, calls=%fused_computation.24 | convolution fusion | flops 12892766208 | bytes 20971520 | tf_op jit(solution)/shard_map/nk,akx->anx/dot_general | solution.py:40
  602.4 11.3 %copy.84 = bf16[2,512,2048]{2,0,1:T(2,128)(2,1)} copy(bf16[2,512,2048]{1,2,0:T(8,128)(2,1)} %fusion.10) | data formatting | bytes 8388608 | tf_op jit(solution)/shard_map/convert_element_type | solution.py:16
  613.7 17.8 %all-to-all-done.7 = bf16[2,512,2048]{2,0,1:T(2,128)(2,1)} async-done(((bf16[2,512,2048]{2,0,1:T(2,128)(2,1)}), bf16[2,512,2048]{2,0,1:T(2,128)(2,1)}, u32[]{:S(2)}, u32[]{:S(2)}) %all-to-all-start.7) | async-done | bytes 4194336 | tf_op jit(solution)/shard_map/all_to_all | solution.py:132
  631.5 19.7 %all-to-all-start.6 = ((bf16[2,512,2048]{2,0,1:T(2,128)(2,1)}), bf16[2,512,2048]{2,0,1:T(2,128)(2,1)}, u32[]{:S(2)}, u32[]{:S(2)}) async-start(bf16[2,512,2048]{2,0,1:T(2,128)(2,1)} %copy.84), calls=%async_computation.6 | async-start | bytes 8388608 | tf_op jit(solution)/shard_map/all_to_all | solution.py:129
  665.2 10.9 %reshape.78 = f32[32,32,2048]{2,0,1:T(8,128)} reshape(f32[16,2,32,2048]{3,1,0,2:T(2,128)} %copy.89) | data formatting | bytes 16777216 | tf_op jit(solution)/shard_map/convert_element_type | solution.py:132
  676.1 52.8 %all-to-all-done.6 = bf16[2,512,2048]{2,0,1:T(2,128)(2,1)} async-done(((bf16[2,512,2048]{2,0,1:T(2,128)(2,1)}), bf16[2,512,2048]{2,0,1:T(2,128)(2,1)}, u32[]{:S(2)}, u32[]{:S(2)}) %all-to-all-start.6) | async-done | bytes 4194336 | tf_op jit(solution)/shard_map/all_to_all | solution.py:129
  742.7 10.9 %reshape.77 = f32[32,32,2048]{2,0,1:T(8,128)} reshape(f32[16,2,32,2048]{3,1,0,2:T(2,128)} %copy.86) | data formatting | bytes 16777216 | tf_op jit(solution)/shard_map/convert_element_type | solution.py:129
  771.4 66.9 %all_to_all.123 = bf16[16,32,2048]{2,1,0:T(8,128)(2,1)} all-to-all(bf16[16,32,2048]{2,1,0:T(8,128)(2,1)S(1)} %copy.90), channel_id=1, replica_groups=mesh['seq'=16,'chan'=2] {'seq'}, dimensions={0} | all-to-all | bytes 4194304 | tf_op jit(solution)/shard_map/all_to_all | solution.py:137
  838.3 26.8 %convolution_convert_fusion = bf16[512,8192]{1,0:T(8,128)(2,1)} fusion(bf16[2048,8192]{1,0:T(8,128)(2,1)} %all-gather.2.cloned.1.call-done, bf16[512,2048]{1,0:T(8,128)(2,1)} %bitcast.173, f32[3,512,2048]{2,1,0:T(8,128)} %copy-done.3, bf16[1,512,2048]{2,1,0:T(8,128)(2,1)S(1)} %copy-done.8, f32[2048]{0:T(1024)S(1)} %copy-done.11), kind=kOutput, calls=%fused_computation.5 | convolution fusion | flops 17191403520 | bytes 48242688 | tf_op jit(solution)/shard_map/dot_general | solution.py:161
  865.1 99.8 %reduce-scatter.2.cloned.1.call-done = bf16[512,4096]{1,0:T(8,128)(2,1)} async-done(((bf16[512,8192]{1,0:T(8,128)(2,1)}), bf16[512,4096]{1,0:T(8,128)(2,1)}) %reduce-scatter.2.cloned.1.call-update) | async-done | bytes 4194320 | tf_op jit(solution)/shard_map/reduce_scatter | solution.py:164
  (85 shorter events, 175.9 us)
Async XLA Ops:
  6.5 17.1 %copy-start.4 = (bf16[512,2048]{1,0:T(8,128)(2,1)S(1)}, bf16[512,2048]{1,0:T(8,128)(2,1)}, u32[]{:S(2)}) copy-start(bf16[512,2048]{1,0:T(8,128)(2,1)} %param.9) | copy-start | bytes 6291460
  6.5 6.8 copy-start.9
  6.5 17.0 %copy-start.10 = (f32[3,3,2048]{2,1,0:T(4,128)S(1)}, f32[3,3,2048]{2,1,0:T(4,128)}, u32[]{:S(2)}) copy-start(f32[3,3,2048]{2,1,0:T(4,128)} %param.10) | copy-start | bytes 221188
  6.5 831.7 %all-gather.2.cloned.1.call-start = ((), (), s32[]{:S(2)}) async-start(), calls=%async_computation.10 | async-start | bytes 35651584 | tf_op jit(solution)/shard_map/all_gather | solution.py:162
  11.0 12.7 %collective-permute-start = (bf16[3,2,2048]{2,1,0:T(2,128)(2,1)S(1)}, bf16[3,2,2048]{2,1,0:T(2,128)(2,1)S(1)}, u32[]{:S(2)}, u32[]{:S(2)}) collective-permute-start(bf16[3,2,2048]{2,1,0:T(2,128)(2,1)S(1)} %slice.37), channel_id=1, source_target_pairs={{0,2},{2,4},{4,6},{6,8},{8,10},{10,12},{12,14},{14,16},{16,18},{18... | collective-permute-start | bytes 73736 | tf_op jit(solution)/shard_map/ppermute | solution.py:22
  16.3 43.1 %all-to-all-start.3 = ((bf16[16,2,2048]{2,1,0:T(2,128)(2,1)}), bf16[16,2,2048]{2,1,0:T(2,128)(2,1)S(1)}, u32[]{:S(2)}, u32[]{:S(2)}) async-start(bf16[16,2,2048]{2,1,0:T(2,128)(2,1)} %reshape.89), calls=%async_computation.3 | async-start | bytes 262144 | tf_op jit(solution)/shard_map/all_to_all | solution.py:98
  23.5 4.5 copy-start.5
  23.5 4.5 copy-start.6
  31.8 4.5 copy-start.3
  36.9 1.4 copy-start.7
  59.4 79.7 %all-to-all-start = ((bf16[16,2,32768]{2,1,0:T(2,128)(2,1)}), bf16[16,2,32768]{2,1,0:T(2,128)(2,1)S(1)}, u32[]{:S(2)}, u32[]{:S(2)}) async-start(bf16[16,2,32768]{2,1,0:T(2,128)(2,1)} %reshape.87), calls=%async_computation | async-start | bytes 4194304 | tf_op jit(solution)/shard_map/all_to_all | solution.py:95
  139.1 20.9 %all-to-all-start.5 = ((bf16[32,32,128]{2,1,0:T(8,128)(2,1)}), bf16[32,32,128]{2,1,0:T(8,128)(2,1)S(1)}, u32[]{:S(2)}, u32[]{:S(2)}) async-start(bf16[32,32,128]{2,1,0:T(8,128)(2,1)} %copy.77), calls=%async_computation.5 | async-start | bytes 524288 | tf_op jit(solution)/shard_map/all_to_all | solution.py:117
  160.0 20.6 %all-to-all-start.4 = ((bf16[32,32,128]{2,1,0:T(8,128)(2,1)}), bf16[32,32,128]{2,1,0:T(8,128)(2,1)S(1)}, u32[]{:S(2)}, u32[]{:S(2)}) async-start(bf16[32,32,128]{2,1,0:T(8,128)(2,1)} %copy.74), calls=%async_computation.4 | async-start | bytes 524288 | tf_op jit(solution)/shard_map/all_to_all | solution.py:114
  180.6 111.6 %all-to-all-start.1 = ((bf16[32,32,2048]{2,1,0:T(8,128)(2,1)}), bf16[32,32,2048]{2,1,0:T(8,128)(2,1)}, u32[]{:S(2)}, u32[]{:S(2)}) async-start(bf16[32,32,2048]{2,1,0:T(8,128)(2,1)} %copy.64), calls=%async_computation.1 | async-start | bytes 8388608 | tf_op jit(solution)/shard_map/all_to_all | solution.py:108
  292.2 114.4 %all-to-all-start.2 = ((bf16[32,32,2048]{2,1,0:T(8,128)(2,1)}), bf16[32,32,2048]{2,1,0:T(8,128)(2,1)}, u32[]{:S(2)}, u32[]{:S(2)}) async-start(bf16[32,32,2048]{2,1,0:T(8,128)(2,1)} %copy.67), calls=%async_computation.2 | async-start | bytes 8388608 | tf_op jit(solution)/shard_map/all_to_all | solution.py:111
  406.6 3.4 copy-start.2
  475.8 23.8 %copy-start = (f32[2,512,2048]{1,2,0:T(8,128)S(1)}, f32[2,512,2048]{1,2,0:T(8,128)}, u32[]{:S(2)}) copy-start(f32[2,512,2048]{1,2,0:T(8,128)} %get-tuple-element.6) | copy-start | bytes 25165828
  533.7 97.8 %all-to-all-start.7 = ((bf16[2,512,2048]{2,0,1:T(2,128)(2,1)}), bf16[2,512,2048]{2,0,1:T(2,128)(2,1)}, u32[]{:S(2)}, u32[]{:S(2)}) async-start(bf16[2,512,2048]{2,0,1:T(2,128)(2,1)} %copy.87), calls=%async_computation.7 | async-start | bytes 8388608 | tf_op jit(solution)/shard_map/all_to_all | solution.py:132
  631.5 97.4 %all-to-all-start.6 = ((bf16[2,512,2048]{2,0,1:T(2,128)(2,1)}), bf16[2,512,2048]{2,0,1:T(2,128)(2,1)}, u32[]{:S(2)}, u32[]{:S(2)}) async-start(bf16[2,512,2048]{2,0,1:T(2,128)(2,1)} %copy.84), calls=%async_computation.6 | async-start | bytes 8388608 | tf_op jit(solution)/shard_map/all_to_all | solution.py:129
  651.2 313.7 %reduce-scatter.2.cloned.1.call-start = ((), (), s32[]{:S(2)}) async-start(), calls=%async_computation.11 | async-start | bytes 12582912 | tf_op jit(solution)/shard_map/reduce_scatter | solution.py:164
  753.5 8.8 copy-start.1
  770.2 68.1 %copy-start.8 = (bf16[1,512,2048]{2,1,0:T(8,128)(2,1)S(1)}, bf16[1,512,2048]{2,1,0:T(8,128)(2,1)}, u32[]{:S(2)}) copy-start(bf16[1,512,2048]{2,1,0:T(8,128)(2,1)} %copy-done.7) | copy-start | bytes 6291460
  770.2 68.0 %copy-start.11 = (f32[2048]{0:T(1024)S(1)}, f32[2048]{0:T(1024)}, u32[]{:S(2)}) copy-start(f32[2048]{0:T(1024)} %param.12) | copy-start | bytes 24580
Sparse Core Ops, SparseCore 0:
  8.9 290.6 all-gather.1
  865.2 99.6 reduce-scatter.1
where the time goes:
time: 982 us; the launch traced here: 972 us
  waiting for transfers between devices  395 us (40%)
  matrix products  242 us (25%)
  local copies, waits for them, and re-layouts  118 us (12%)
  starting transfers between devices  107 us (11%)
  blocking collectives  66.9 us (7%)
  other arithmetic  29.2 us (3%)
  between operations  14.3 us (1%)
    dot_general x18, matrix products, apply_table(): return jnp.einsum(form, table, data, precision=HIGHEST)  215 us
    reduce_scatter x1, waiting for transfers between devices, on_device(): lax.psum_scatter(terms.astype(jnp.bfloat16), 'chan', scatter_dimension=1,...  99.8 us
    all_to_all x1, waiting for transfers between devices, spread_conv(): lax.all_to_all(data_re.astype(jnp.bfloat16), 'seq', split_axis=0, concat_...  99.7 us
    all_to_all x1, waiting for transfers between devices, spread_conv(): lax.all_to_all(gated[None], 'seq', split_axis=1, concat_axis=0, tiled=True)  71.3 us
    all_to_all x1, blocking collectives, spread_conv(): lax.all_to_all(result, 'seq', split_axis=0, concat_axis=1, tiled=True)[0]  66.9 us
    all_to_all x1, waiting for transfers between devices, spread_conv(): lax.all_to_all(as_sent(back_re), 'seq', split_axis=1, concat_axis=0, tile...  52.8 us
    all_to_all x1, waiting for transfers between devices, spread_conv(): lax.all_to_all(data_im.astype(jnp.bfloat16), 'seq', split_axis=0, concat_...  51.9 us
    all_to_all x1, starting transfers between devices, spread_conv(): lax.all_to_all(data_im.astype(jnp.bfloat16), 'seq', split_axis=0, concat_...  36.7 us
  transfers between devices with their start and end apart: 11, of which 7 were waited for; matrix products, arithmetic and copies ran while one was open for 37% of the time, Pallas kernels for 0%

commit v1 on v0

v1 whole, which is shorter than its diff:
```python
import functools

import jax
import jax.numpy as jnp
from jax import lax
from jax.experimental import pallas as pl
from jax.experimental.pallas import tpu as pltpu
from jax.sharding import PartitionSpec as P

GROUP = 16
KW = 3
BLOCK = 256
TILE = 128


def short_taps(x, border, taps):
    rows = x.shape[0]
    extended = jnp.concatenate([border, x.astype(jnp.float32)], axis=0)
    first = border.shape[0]
    total = taps[0:1] * extended[first:]
    for shift in range(1, KW):
        total = total + taps[shift : shift + 1] * extended[first - shift : first - shift + rows]
    return total


def front_kernel(q_ref, k_ref, v_ref, border_ref, taps_ref, query_ref, gated_ref):
    query = short_taps(q_ref[...], border_ref[0], taps_ref[0])
    key = short_taps(k_ref[...], border_ref[1], taps_ref[1])
    value = short_taps(v_ref[...], border_ref[2], taps_ref[2])
    query_ref[...] = query.T.astype(jnp.bfloat16)
    gated_ref[...] = (key * value).T.astype(jnp.bfloat16)


def front(query_in, key_in, value_in, border, taps):
    rows, width = query_in.shape
    wide = min(width, 256)
    signal = pl.BlockSpec((rows, wide), lambda i: (0, i))
    turned = pl.BlockSpec((wide, rows), lambda i: (i, 0))
    return pl.pallas_call(
        front_kernel,
        grid=(width // wide,),
        in_specs=[
            signal,
            signal,
            signal,
            pl.BlockSpec((3, 8, wide), lambda i: (0, 0, i)),
            pl.BlockSpec((3, KW, wide), lambda i: (0, 0, i)),
        ],
        out_specs=[turned, turned],
        out_shape=[jax.ShapeDtypeStruct((width, rows), jnp.bfloat16)] * 2,
        compiler_params=pltpu.CompilerParams(vmem_limit_bytes=32 * 1024 * 1024),
        cost_estimate=pl.CostEstimate(
            flops=20 * rows * width, bytes_accessed=10 * rows * width, transcendentals=0
        ),
    )(query_in, key_in, value_in, border, taps)


def conv_kernel(parts, blocks, data_ref, lags_ref, out_ref, held, toeplitz, total):
    local_len = data_ref.shape[2]
    per = local_len // BLOCK
    rows = blocks * GROUP
    held[0:rows, :] = jnp.zeros((rows, BLOCK), held.dtype)
    for part in range(parts):
        for piece in range(per):
            at = rows + (part * per + piece) * GROUP
            held[at : at + GROUP, :] = data_ref[part, :, piece * BLOCK : (piece + 1) * BLOCK]

    tiles = toeplitz.shape[0]

    def build(m, carry):
        line = jnp.broadcast_to(lags_ref[0, pl.ds(m, 1), :], (TILE, 2 * TILE))
        turned = pltpu.roll(line, 0, 1, stride=1, stride_axis=0)
        toeplitz[pl.ds(m, 1)] = turned[:, TILE:].astype(jnp.bfloat16)[None]
        return carry

    lax.fori_loop(0, tiles, build, 0)
    total[...] = jnp.zeros_like(total)
    half = rows // 2

    def weights(k):
        now = toeplitz[2 * k + 1]
        return jnp.concatenate(
            [
                jnp.concatenate([now, toeplitz[2 * k + 2]], axis=1),
                jnp.concatenate([toeplitz[2 * k], now], axis=1),
            ],
            axis=0,
        )

    def near(k, carry):
        start = pl.multiple_of(rows - k * GROUP, GROUP)
        total[...] += jnp.dot(
            held[pl.ds(start, rows), :], weights(k), preferred_element_type=jnp.float32
        )
        return carry

    def far(k, carry):
        start = pl.multiple_of(rows + half - k * GROUP, GROUP)
        total[half:, :] += jnp.dot(
            held[pl.ds(start, half), :], weights(k), preferred_element_type=jnp.float32
        )
        return carry

    lax.fori_loop(0, blocks // 2, near, 0)
    lax.fori_loop(blocks // 2, blocks, far, 0)
    for part in range(parts):
        for piece in range(per):
            at = (part * per + piece) * GROUP
            out_ref[part, :, piece * BLOCK : (piece + 1) * BLOCK] = total[
                at : at + GROUP, :
            ].astype(jnp.bfloat16)


def long_conv(data, lags):
    parts, channels, local_len = data.shape
    groups, tiles, _ = lags.shape
    blocks = parts * local_len // BLOCK
    rows = blocks * GROUP
    return pl.pallas_call(
        functools.partial(conv_kernel, parts, blocks),
        grid=(groups,),
        in_specs=[
            pl.BlockSpec((parts, GROUP, local_len), lambda g: (0, g, 0)),
            pl.BlockSpec((1, tiles, 2 * TILE), lambda g: (g, 0, 0)),
        ],
        out_specs=pl.BlockSpec((parts, GROUP, local_len), lambda g: (0, g, 0)),
        out_shape=jax.ShapeDtypeStruct(data.shape, jnp.bfloat16),
        scratch_shapes=[
            pltpu.VMEM((2 * rows, BLOCK), jnp.bfloat16),
            pltpu.VMEM((tiles, TILE, TILE), jnp.bfloat16),
            pltpu.VMEM((rows, BLOCK), jnp.float32),
        ],
        compiler_params=pltpu.CompilerParams(vmem_limit_bytes=32 * 1024 * 1024),
        cost_estimate=pl.CostEstimate(
            flops=2 * groups * blocks * rows * BLOCK * BLOCK,
            bytes_accessed=4 * parts * channels * local_len,
            transcendentals=0,
        ),
    )(data, lags)


def on_device(query_in, key_in, value_in, short_weight, long_filter, skip_gain, w_out):
    local_len, width = query_in.shape
    parts = lax.axis_size("seq")
    slabs = lax.axis_size("chan")
    chan = lax.axis_index("chan")
    columns = w_out.shape[1]
    chunk = 128
    gathered = [
        lax.all_gather(w_out[:, at : at + chunk], "seq", axis=1, tiled=True)
        for at in range(0, columns, chunk)
    ]

    filt = lax.all_to_all(
        long_filter.astype(jnp.bfloat16).reshape(parts, -1, local_len),
        "seq",
        split_axis=0,
        concat_axis=0,
        tiled=True,
    )
    groups = filt.shape[1]
    filt = jnp.transpose(filt, (1, 0, 2)).reshape(groups, -1, TILE).astype(jnp.float32)
    now = jnp.pad(filt, ((0, 0), (1, 0), (0, 0)))
    before = jnp.pad(filt[:, :-1], ((0, 0), (2, 0), (0, 0)))
    lags = jnp.concatenate([before, now], axis=2)

    ends = jnp.stack([a[local_len - (KW - 1) :] for a in (query_in, key_in, value_in)])
    border = lax.ppermute(ends, "seq", [(i, i + 1) for i in range(parts - 1)])
    border = jnp.pad(border.astype(jnp.float32), ((0, 0), (8 - (KW - 1), 0), (0, 0)))
    query_conv, gated = front(query_in, key_in, value_in, border, short_weight)
    moved = lax.all_to_all(
        gated.reshape(parts, -1, local_len), "seq", split_axis=0, concat_axis=0, tiled=True
    )
    conv = long_conv(moved, lags)
    conv = lax.all_to_all(conv, "seq", split_axis=0, concat_axis=0, tiled=True)
    conv = conv.reshape(width, local_len)
    mixed = (
        query_conv.astype(jnp.float32)
        * (conv.astype(jnp.float32) + skip_gain[:, None] * gated.astype(jnp.float32))
    ).astype(jnp.bfloat16)
    mixed = lax.optimization_barrier(mixed.T)

    outs = []
    for weights in gathered:
        terms = jnp.dot(mixed, weights, preferred_element_type=jnp.float32).astype(jnp.bfloat16)
        if slabs == 2:
            own = terms.shape[1] // 2
            sent = lax.dynamic_slice_in_dim(terms, (1 - chan) * own, own, 1)
            kept = lax.dynamic_slice_in_dim(terms, chan * own, own, 1)
            got = lax.ppermute(sent, "chan", [(0, 1), (1, 0)])
            summed = (kept.astype(jnp.float32) + got.astype(jnp.float32)).astype(jnp.bfloat16)
        else:
            summed = lax.psum_scatter(terms, "chan", scatter_dimension=1, tiled=True)
        outs.append(summed.reshape(local_len, -1, chunk))
    return jnp.stack(outs, axis=2).reshape(local_len, -1)


def solution(mesh):
    placed = (
        P("seq", "chan"),
        P("seq", "chan"),
        P("seq", "chan"),
        P(None, None, "chan"),
        P("chan", "seq"),
        P("chan"),
        P("chan", "seq"),
    )
    return jax.shard_map(
        on_device, mesh=mesh, in_specs=placed, out_specs=P("seq", "chan"), check_vma=False
    )
```

time: 982 us -> 462 us (0.47)
  matrix products: 242 us -> 33.3 us
  waiting for transfers between devices: 395 us -> 212 us
  Pallas kernels: 0 us -> 109 us
  local copies, waits for them, and re-layouts: 118 us -> 34.8 us
  blocking collectives: 66.9 us -> 0 us
  starting transfers between devices: 107 us -> 45.4 us
  other arithmetic: 29.2 us -> 12.8 us
    dot_general x19 -> x4, matrix products: 242 us -> 33.3 us  [on_device(): jnp.dot(mixed, weights, preferred_element_type=jnp.float32)]
    all_to_all x8 -> x3, waiting for transfers between devices: 294 us -> 128 us  [the longest x1 65.5 us: on_device(): conv = lax.all_to_all(conv, 'seq', split_axis=0, concat_axis=0, tiled=True)]
    pallas_call x0 -> x2, Pallas kernels: none -> 109 us  [the longest x1 101 us: long_conv(): pl.pallas_call(functools.partial(conv_kernel, parts, blocks), grid=(group...]
    reduce_scatter x1 -> x0, waiting for transfers between devices: 99.8 us -> none  [on_device(): lax.psum_scatter(terms.astype(jnp.bfloat16), 'chan', scatter_dimension=1,...]
    convert_element_type x13 -> x2, local copies, waits for them, and re-layouts: 80.8 us -> 0.18 us  [on_device(): jnp.transpose(filt, (1, 0, 2)).reshape(groups, -1, TILE).astype(jnp.float32)]
    all_to_all x8 -> x3, starting transfers between devices: 105 us -> 38 us  [the longest x1 24.8 us: on_device(): conv = lax.all_to_all(conv, 'seq', split_axis=0, concat_axis=0, tiled=True)]
    all_to_all x1 -> x0, blocking collectives: 66.9 us -> none  [spread_conv(): lax.all_to_all(result, 'seq', split_axis=0, concat_axis=1, tiled=True)[0]]
    all_gather x1 -> x4, waiting for transfers between devices: 0.01 us -> 64.2 us  [on_device(): lax.all_gather(w_out[:, at:at + chunk], 'seq', axis=1, tiled=True)]
  transfers between devices with their start and end apart: 11 -> 12, of which waited for: 7 -> 4; matrix products, arithmetic and copies ran while one was open for 37% -> 11% of each run, Pallas kernels for 0% -> 24%
where the time goes in v1:
time: 462 us; the launch traced here: 461 us
  waiting for transfers between devices  212 us (46%)
  Pallas kernels  109 us (24%)
  starting transfers between devices  45.4 us (10%)
  local copies, waits for them, and re-layouts  34.8 us (8%)
  matrix products  33.3 us (7%)
  between operations  13.5 us (3%)
  other arithmetic  12.8 us (3%)
    pallas_call x1, Pallas kernels, long_conv(): pl.pallas_call(functools.partial(conv_kernel, parts, blocks), grid=(group...  101 us
    all_to_all x1, waiting for transfers between devices, on_device(): conv = lax.all_to_all(conv, 'seq', split_axis=0, concat_axis=0, tiled=True)  65.5 us
    all_gather x4, waiting for transfers between devices, on_device(): lax.all_gather(w_out[:, at:at + chunk], 'seq', axis=1, tiled=True)  64.2 us
    all_to_all x1, waiting for transfers between devices, on_device(): lax.all_to_all(gated.reshape(parts, -1, local_len), 'seq', split_axis=0,...  62.7 us
    dot_general x4, matrix products, on_device(): jnp.dot(mixed, weights, preferred_element_type=jnp.float32)  33.3 us
    all_to_all x1, starting transfers between devices, on_device(): conv = lax.all_to_all(conv, 'seq', split_axis=0, concat_axis=0, tiled=True)  24.8 us
    ppermute x4, waiting for transfers between devices, on_device(): got = lax.ppermute(sent, 'chan', [(0, 1), (1, 0)])  17.9 us
    unnamed x40, local copies, waits for them, and re-layouts  12.3 us
  transfers between devices with their start and end apart: 12, of which 4 were waited for; matrix products, arithmetic and copies ran while one was open for 11% of the time, Pallas kernels for 24%

profile of v1, /device:TPU:0, one launch (start us, length us, event | category | flops | bytes accessed | tf_op | source)
XLA Modules:
  0.0 460.8 jit_solution(13379294431284248081)
XLA Ops:
  6.5 2.9 fusion.7
  12.5 2.4 collective-permute-start
  15.5 7.2 %all-to-all-start.1 = ((bf16[16,8,512]{2,1,0:T(8,128)(2,1)}), bf16[16,8,512]{2,1,0:T(8,128)(2,1)S(1)}, u32[]{:S(2)}, u32[]{:S(2)}) async-start(bf16[16,8,512]{2,1,0:T(8,128)(2,1)} %convert_bitcast_fusion.1), calls=%async_computation.1 | async-start | bytes 262144 | tf_op jit(solution)/shard_map/all_to_all | solution.py:154
  22.8 1.6 copy-done.1
  24.4 1.6 copy-done.2
  25.9 7.4 %shard_map.73 = (bf16[2048,512]{1,0:T(8,128)(2,1)S(1)}, bf16[2048,512]{1,0:T(8,128)(2,1)}) custom-call(bf16[512,2048]{1,0:T(8,128)(2,1)S(1)} %copy-done, bf16[512,2048]{1,0:T(8,128)(2,1)S(1)} %copy-done.1, bf16[512,2048]{1,0:T(8,128)(2,1)S(1)} %copy-done.2, f32[3,8,2048]{2,1,0:T(8,128)S(1)} %pad_convert_fusion.border_ref, f32[3,3,2048]{2,1,0:T(4,128)S(1)} %copy-done.6), custom_call_target="tpu_custom_call" | custom-call | flops 20971520 | bytes 10485760 | tf_op jit(solution)/shard_map/pallas_call | solution.py:39
  34.7 6.0 %all-to-all-start = ((bf16[16,128,512]{2,1,0:T(8,128)(2,1)}), bf16[16,128,512]{2,1,0:T(8,128)(2,1)S(1)}, u32[]{:S(2)}, u32[]{:S(2)}) async-start(bf16[16,128,512]{2,1,0:T(8,128)(2,1)} %bitcast.3), calls=%async_computation | async-start | bytes 4194304 | tf_op jit(solution)/shard_map/all_to_all | solution.py:171
  41.0 62.7 %all-to-all-done.data_ref = bf16[16,128,512]{2,1,0:T(8,128)(2,1)S(1)} async-done(((bf16[16,128,512]{2,1,0:T(8,128)(2,1)}), bf16[16,128,512]{2,1,0:T(8,128)(2,1)S(1)}, u32[]{:S(2)}, u32[]{:S(2)}) %all-to-all-start) | async-done | bytes 2097184 | tf_op jit(solution)/shard_map/all_to_all | solution.py:171
  103.6 101.4 %shard_map.74 = bf16[16,128,512]{2,1,0:T(8,128)(2,1)S(1)} custom-call(bf16[16,128,512]{2,1,0:T(8,128)(2,1)S(1)} %all-to-all-done.data_ref, f32[8,65,256]{2,1,0:T(8,128)S(1)} %select_maximum_fusion.lags_ref), custom_call_target="tpu_custom_call" | custom-call | flops 17179869184 | bytes 4194304 | tf_op jit(solution)/shard_map/pallas_call | solution.py:119
  206.4 24.8 %all-to-all-start.2 = ((bf16[16,128,512]{2,1,0:T(8,128)(2,1)}), bf16[16,128,512]{2,1,0:T(8,128)(2,1)}, u32[]{:S(2)}, u32[]{:S(2)}) async-start(bf16[16,128,512]{2,1,0:T(8,128)(2,1)} %copy-done.5), calls=%async_computation.2 | async-start | bytes 4194304 | tf_op jit(solution)/shard_map/all_to_all | solution.py:175
  231.1 65.5 %all-to-all-done.2 = bf16[16,128,512]{2,1,0:T(8,128)(2,1)} async-done(((bf16[16,128,512]{2,1,0:T(8,128)(2,1)}), bf16[16,128,512]{2,1,0:T(8,128)(2,1)}, u32[]{:S(2)}, u32[]{:S(2)}) %all-to-all-start.2) | async-done | bytes 2097184 | tf_op jit(solution)/shard_map/all_to_all | solution.py:175
  296.6 4.5 fusion.2
  301.1 8.7 %convolution_convert_fusion.3 = bf16[512,2048]{1,0:T(8,128)(2,1)S(1)} fusion(bf16[512,2048]{0,1:T(8,128)(2,1)} %fusion.2, bf16[2048,2048]{1,0:T(8,128)(2,1)} %all-gather.5.cloned.1.call-done), kind=kOutput, calls=%fused_computation.7 | convolution fusion | flops 4296015872 | bytes 12582912 | tf_op jit(solution)/shard_map/dot_general | solution.py:185
  312.8 8.1 %convolution_convert_fusion.2 = bf16[512,2048]{1,0:T(8,128)(2,1)S(1)} fusion(bf16[512,2048]{0,1:T(8,128)(2,1)S(1)} %copy-done.7, bf16[2048,2048]{1,0:T(8,128)(2,1)} %all-gather.7.cloned.1.call-done), kind=kOutput, calls=%fused_computation.6 | convolution fusion | flops 4296015872 | bytes 12582912 | tf_op jit(solution)/shard_map/dot_general | solution.py:185
  324.8 8.1 %convolution_convert_fusion.1 = bf16[512,2048]{1,0:T(8,128)(2,1)S(1)} fusion(bf16[512,2048]{0,1:T(8,128)(2,1)S(1)} %copy-done.7, bf16[2048,2048]{1,0:T(8,128)(2,1)} %all-gather.9.cloned.1.call-done), kind=kOutput, calls=%fused_computation.5 | convolution fusion | flops 4296015872 | bytes 12582912 | tf_op jit(solution)/shard_map/dot_general | solution.py:185
  336.1 64.1 %all-gather.11.cloned.1.call-done = bf16[2048,2048]{1,0:T(8,128)(2,1)} async-done(((bf16[2048,128]{1,0:T(8,128)(2,1)}), bf16[2048,2048]{1,0:T(8,128)(2,1)}) %all-gather.11.cloned.1.call-update) | async-done | bytes 8388624 | tf_op jit(solution)/shard_map/all_gather | solution.py:150
  400.2 8.4 %convolution_convert_fusion = bf16[512,2048]{1,0:T(8,128)(2,1)S(1)} fusion(bf16[512,2048]{0,1:T(8,128)(2,1)S(1)} %copy-done.7, bf16[2048,2048]{1,0:T(8,128)(2,1)} %all-gather.11.cloned.1.call-done), kind=kOutput, calls=%fused_computation.4 | convolution fusion | flops 4296015872 | bytes 12582912 | tf_op jit(solution)/shard_map/dot_general | solution.py:185
  412.5 1.8 fusion.3
  414.6 1.8 fusion.4
  416.6 1.8 fusion.5
  418.7 17.9 %collective-permute-done.4 = bf16[512,1024]{1,0:T(8,128)(2,1)} collective-permute-done((bf16[512,1024]{1,0:T(8,128)(2,1)}, bf16[512,1024]{1,0:T(8,128)(2,1)}, u32[]{:S(2)}, u32[]{:S(2)}) %collective-permute-start.4) | collective-permute-done | bytes 1048608 | tf_op jit(solution)/shard_map/ppermute | solution.py:190
  436.6 1.6 fusion.6
  439.1 7.4 %copy.11 = bf16[512,8,4,128]{3,2,1,0:T(4,128)(2,1)} copy(bf16[512,8,4,128]{3,1,0,2:T(8,128)(2,1)S(1)} %pad_maximum_fusion) | data formatting | bytes 8388608 | tf_op jit(solution)/shard_map/stack | solution.py:195
  446.5 7.8 %reshape.18 = bf16[512,4096]{1,0:T(8,128)(2,1)} reshape(bf16[512,8,4,128]{3,2,1,0:T(4,128)(2,1)} %copy.11) | data formatting | bytes 8388608 | tf_op jit(solution)/shard_map/reshape | solution.py:195
  (72 shorter events, 21.9 us)
Async XLA Ops:
  6.5 294.6 %all-gather.5.cloned.1.call-start = ((), (), s32[]{:S(2)}) async-start(), calls=%async_computation.3 | async-start | bytes 8912896 | tf_op jit(solution)/shard_map/all_gather | solution.py:150
  6.5 8.3 %copy-start.16 = (f32[128,512]{1,0:T(8,128)S(1)}, f32[128,512]{1,0:T(8,128)}, u32[]{:S(2)}) copy-start(f32[128,512]{1,0:T(8,128)} %param.11) | copy-start | bytes 786436
  9.5 2.1 copy-start
  9.5 13.3 %copy-start.6 = (f32[3,3,2048]{2,1,0:T(4,128)S(1)}, f32[3,3,2048]{2,1,0:T(4,128)}, u32[]{:S(2)}) copy-start(f32[3,3,2048]{2,1,0:T(4,128)} %taps_ref.1) | copy-start | bytes 221188
  9.5 303.3 %all-gather.7.cloned.1.call-start = ((), (), s32[]{:S(2)}) async-start(), calls=%async_computation.4 | async-start | bytes 8912896 | tf_op jit(solution)/shard_map/all_gather | solution.py:150
  10.3 314.6 %all-gather.9.cloned.1.call-start = ((), (), s32[]{:S(2)}) async-start(), calls=%async_computation.5 | async-start | bytes 8912896 | tf_op jit(solution)/shard_map/all_gather | solution.py:150
  11.0 389.2 %all-gather.11.cloned.1.call-start = ((), (), s32[]{:S(2)}) async-start(), calls=%async_computation.6 | async-start | bytes 8912896 | tf_op jit(solution)/shard_map/all_gather | solution.py:150
  12.5 10.2 %collective-permute-start = (bf16[3,2,2048]{2,1,0:T(2,128)(2,1)S(1)}, bf16[3,2,2048]{2,1,0:T(2,128)(2,1)S(1)}, u32[]{:S(2)}, u32[]{:S(2)}) collective-permute-start(bf16[3,2,2048]{2,1,0:T(2,128)(2,1)S(1)} %pad_maximum_fusion.1), channel_id=1, source_target_pairs={{0,2},{2,4},{4,6},{6,8},{8,10},{10,12},{12,14},{14,16},{16,18},{18... | collective-permute-start | bytes 73736 | tf_op jit(solution)/shard_map/ppermute | solution.py:168
  15.5 19.2 %all-to-all-start.1 = ((bf16[16,8,512]{2,1,0:T(8,128)(2,1)}), bf16[16,8,512]{2,1,0:T(8,128)(2,1)S(1)}, u32[]{:S(2)}, u32[]{:S(2)}) async-start(bf16[16,8,512]{2,1,0:T(8,128)(2,1)} %convert_bitcast_fusion.1), calls=%async_computation.1 | async-start | bytes 262144 | tf_op jit(solution)/shard_map/all_to_all | solution.py:154
  22.8 1.6 copy-start.1
  24.4 1.6 copy-start.2
  34.7 69.0 %all-to-all-start = ((bf16[16,128,512]{2,1,0:T(8,128)(2,1)}), bf16[16,128,512]{2,1,0:T(8,128)(2,1)S(1)}, u32[]{:S(2)}, u32[]{:S(2)}) async-start(bf16[16,128,512]{2,1,0:T(8,128)(2,1)} %bitcast.3), calls=%async_computation | async-start | bytes 4194304 | tf_op jit(solution)/shard_map/all_to_all | solution.py:171
  206.4 90.3 %copy-start.4 = (bf16[2048,512]{1,0:T(8,128)(2,1)S(1)}, bf16[2048,512]{1,0:T(8,128)(2,1)}, u32[]{:S(2)}) copy-start(bf16[2048,512]{1,0:T(8,128)(2,1)} %copy-done.3) | copy-start | bytes 6291460
  206.4 90.3 %copy-start.17 = (f32[2048]{0:T(1024)S(1)}, f32[2048]{0:T(1024)}, u32[]{:S(2)}) copy-start(f32[2048]{0:T(1024)} %param.12) | copy-start | bytes 24580
  206.4 90.3 %all-to-all-start.2 = ((bf16[16,128,512]{2,1,0:T(8,128)(2,1)}), bf16[16,128,512]{2,1,0:T(8,128)(2,1)}, u32[]{:S(2)}, u32[]{:S(2)}) async-start(bf16[16,128,512]{2,1,0:T(8,128)(2,1)} %copy-done.5), calls=%async_computation.2 | async-start | bytes 4194304 | tf_op jit(solution)/shard_map/all_to_all | solution.py:175
  311.2 1.6 copy-start.7
  311.3 101.2 %collective-permute-start.1 = (bf16[512,1024]{1,0:T(8,128)(2,1)S(1)}, bf16[512,1024]{1,0:T(8,128)(2,1)}, u32[]{:S(2)}, u32[]{:S(2)}) collective-permute-start(bf16[512,1024]{1,0:T(8,128)(2,1)S(1)} %constant_dynamic-slice_fusion.3), channel_id=1, source_target_pairs={{0,1},{1,0},{2,3},{3,2},{4,5},{5,4},{6,7},{7,6},{8,9},{9,8},{10,11... | collective-permute-start | bytes 3145736 | tf_op jit(solution)/shard_map/ppermute | solution.py:190
  323.4 91.1 %collective-permute-start.2 = (bf16[512,1024]{1,0:T(8,128)(2,1)}, bf16[512,1024]{1,0:T(8,128)(2,1)}, u32[]{:S(2)}, u32[]{:S(2)}) collective-permute-start(bf16[512,1024]{1,0:T(8,128)(2,1)} %constant_dynamic-slice_fusion.2), channel_id=1, source_target_pairs={{0,1},{1,0},{2,3},{3,2},{4,5},{5,4},{6,7},{7,6},{8,9},{9,8},{10,11... | collective-permute-start | bytes 3145736 | tf_op jit(solution)/shard_map/ppermute | solution.py:190
  335.5 81.2 %collective-permute-start.3 = (bf16[512,1024]{1,0:T(8,128)(2,1)}, bf16[512,1024]{1,0:T(8,128)(2,1)}, u32[]{:S(2)}, u32[]{:S(2)}) collective-permute-start(bf16[512,1024]{1,0:T(8,128)(2,1)} %constant_dynamic-slice_fusion.1), channel_id=1, source_target_pairs={{0,1},{1,0},{2,3},{3,2},{4,5},{5,4},{6,7},{7,6},{8,9},{9,8},{10,11... | collective-permute-start | bytes 3145736 | tf_op jit(solution)/shard_map/ppermute | solution.py:190
  409.9 2.6 copy-start.9
  411.0 25.6 %collective-permute-start.4 = (bf16[512,1024]{1,0:T(8,128)(2,1)}, bf16[512,1024]{1,0:T(8,128)(2,1)}, u32[]{:S(2)}, u32[]{:S(2)}) collective-permute-start(bf16[512,1024]{1,0:T(8,128)(2,1)} %constant_dynamic-slice_fusion), channel_id=1, source_target_pairs={{0,1},{1,0},{2,3},{3,2},{4,5},{5,4},{6,7},{7,6},{8,9},{9,8},{10,11... | collective-permute-start | bytes 3145736 | tf_op jit(solution)/shard_map/ppermute | solution.py:190
  412.5 2.1 copy-start.11
  414.5 2.1 copy-start.13
  416.6 20.0 %copy-start.15 = (bf16[512,2048]{1,0:T(8,128)(2,1)S(1)}, bf16[512,2048]{1,0:T(8,128)(2,1)}, u32[]{:S(2)}) copy-start(bf16[512,2048]{1,0:T(8,128)(2,1)} %copy-done.14) | copy-start | bytes 6291460
  (6 other events, 8.0 us)
Sparse Core Ops, SparseCore 0:
  9.6 118.2 all-gather.4
  130.1 77.4 all-gather.6
  209.7 112.5 all-gather.8
  324.3 75.8 all-gather.10

commit v2 on v1

--- a/solution.py
+++ b/solution.py
@@ -11,6 +11,7 @@
 KW = 3
 BLOCK = 256
 TILE = 128
+RUN = 8
 
 
 def short_taps(x, border, taps):
@@ -65,15 +66,18 @@
             at = rows + (part * per + piece) * GROUP
             held[at : at + GROUP, :] = data_ref[part, :, piece * BLOCK : (piece + 1) * BLOCK]
 
-    tiles = toeplitz.shape[0]
-
-    def build(m, carry):
-        line = jnp.broadcast_to(lags_ref[0, pl.ds(m, 1), :], (TILE, 2 * TILE))
-        turned = pltpu.roll(line, 0, 1, stride=1, stride_axis=0)
-        toeplitz[pl.ds(m, 1)] = turned[:, TILE:].astype(jnp.bfloat16)[None]
+    toeplitz[0] = jnp.zeros((TILE, TILE), toeplitz.dtype)
+    wide = (RUN + 1) * TILE
+
+    def build(step, carry):
+        line = jnp.broadcast_to(lags_ref[0, pl.ds(step, 1), :], (TILE, wide))
+        turned = pltpu.roll(line, 0, 1, stride=1, stride_axis=0).astype(jnp.bfloat16)
+        for tile in range(RUN):
+            at = (tile + 1) * TILE
+            toeplitz[pl.ds(step * RUN + tile + 1, 1)] = turned[:, at : at + TILE][None]
         return carry
 
-    lax.fori_loop(0, tiles, build, 0)
+    lax.fori_loop(0, lags_ref.shape[1], build, 0)
     total[...] = jnp.zeros_like(total)
     half = rows // 2
 
@@ -87,22 +91,26 @@
             axis=0,
         )
 
-    def near(k, carry):
-        start = pl.multiple_of(rows - k * GROUP, GROUP)
-        total[...] += jnp.dot(
-            held[pl.ds(start, rows), :], weights(k), preferred_element_type=jnp.float32
+    def lagged(first, count, k):
+        signal = [
+            held[pl.ds(pl.multiple_of(first - lag * GROUP, GROUP), count), :] for lag in (k, k + 1)
+        ]
+        return jnp.dot(
+            jnp.concatenate(signal, axis=1),
+            jnp.concatenate([weights(k), weights(k + 1)], axis=0),
+            preferred_element_type=jnp.float32,
         )
+
+    def near(step, carry):
+        total[...] += lagged(rows, rows, 2 * step)
         return carry
 
-    def far(k, carry):
-        start = pl.multiple_of(rows + half - k * GROUP, GROUP)
-        total[half:, :] += jnp.dot(
-            held[pl.ds(start, half), :], weights(k), preferred_element_type=jnp.float32
-        )
+    def far(step, carry):
+        total[half:, :] += lagged(rows + half, half, 2 * step)
         return carry
 
-    lax.fori_loop(0, blocks // 2, near, 0)
-    lax.fori_loop(blocks // 2, blocks, far, 0)
+    lax.fori_loop(0, blocks // 4, near, 0)
+    lax.fori_loop(blocks // 4, blocks // 2, far, 0)
     for part in range(parts):
         for piece in range(per):
             at = (part * per + piece) * GROUP
@@ -113,7 +121,8 @@
 
 def long_conv(data, lags):
     parts, channels, local_len = data.shape
-    groups, tiles, _ = lags.shape
+    groups, runs, wide = lags.shape
+    tiles = runs * RUN + 1
     blocks = parts * local_len // BLOCK
     rows = blocks * GROUP
     return pl.pallas_call(
@@ -121,7 +130,7 @@
         grid=(groups,),
         in_specs=[
             pl.BlockSpec((parts, GROUP, local_len), lambda g: (0, g, 0)),
-            pl.BlockSpec((1, tiles, 2 * TILE), lambda g: (g, 0, 0)),
+            pl.BlockSpec((1, runs, wide), lambda g: (g, 0, 0)),
         ],
         out_specs=pl.BlockSpec((parts, GROUP, local_len), lambda g: (0, g, 0)),
         out_shape=jax.ShapeDtypeStruct(data.shape, jnp.bfloat16),
@@ -139,6 +148,45 @@
     )(data, lags)
 
 
+def join_kernel(shape, chunk, core_ref, *refs):
+    chunks, addends, pairs = shape
+    out_ref = refs[-1]
+
+    def place(core):
+        for at in range(chunks):
+            for side in range(2):
+                first = (at * 2 + side) * addends
+                for pair in range(pairs):
+                    cols = slice(pair * chunk, (pair + 1) * chunk)
+                    total = refs[first][:, cols]
+                    if addends == 2:
+                        more = refs[first + 1][:, cols].astype(jnp.float32)
+                        total = (total.astype(jnp.float32) + more).astype(jnp.bfloat16)
+                    owner = pair * 2 + (core + side) % 2
+                    to = (owner * chunks + at) * chunk
+                    out_ref[:, to : to + chunk] = total
+
+    for core in range(2):
+        pl.when(core_ref[0] == core)(functools.partial(place, core))
+
+
+def join(core, pieces, local_len, chunk):
+    flat = [array for both in pieces for side in both for array in side]
+    addends = len(pieces[0][0])
+    wide = flat[0].shape[1]
+    rows = 128
+    total = 2 * len(pieces) * wide
+    return pl.pallas_call(
+        functools.partial(join_kernel, (len(pieces), addends, wide // chunk), chunk),
+        grid=(local_len // rows,),
+        in_specs=[pl.BlockSpec(memory_space=pltpu.SMEM)]
+        + [pl.BlockSpec((rows, wide), lambda i: (i, 0))] * len(flat),
+        out_specs=pl.BlockSpec((rows, total), lambda i: (i, 0)),
+        out_shape=jax.ShapeDtypeStruct((local_len, total), jnp.bfloat16),
+        compiler_params=pltpu.CompilerParams(vmem_limit_bytes=32 * 1024 * 1024),
+    )(core, *flat)
+
+
 def on_device(query_in, key_in, value_in, short_weight, long_filter, skip_gain, w_out):
     local_len, width = query_in.shape
     parts = lax.axis_size("seq")
@@ -146,8 +194,11 @@
     chan = lax.axis_index("chan")
     columns = w_out.shape[1]
     chunk = 128
+    same_core = [list(range(core, parts, 2)) for core in range(2)]
     gathered = [
-        lax.all_gather(w_out[:, at : at + chunk], "seq", axis=1, tiled=True)
+        lax.all_gather(
+            w_out[:, at : at + chunk], "seq", axis=1, tiled=True, axis_index_groups=same_core
+        )
         for at in range(0, columns, chunk)
     ]
 
@@ -159,10 +210,9 @@
         tiled=True,
     )
     groups = filt.shape[1]
-    filt = jnp.transpose(filt, (1, 0, 2)).reshape(groups, -1, TILE).astype(jnp.float32)
-    now = jnp.pad(filt, ((0, 0), (1, 0), (0, 0)))
-    before = jnp.pad(filt[:, :-1], ((0, 0), (2, 0), (0, 0)))
-    lags = jnp.concatenate([before, now], axis=2)
+    filt = jnp.transpose(filt, (1, 0, 2)).reshape(groups, -1, RUN * TILE).astype(jnp.float32)
+    before = jnp.pad(filt[:, :-1, -TILE:], ((0, 0), (1, 0), (0, 0)))
+    lags = jnp.concatenate([before, filt], axis=2)
 
     ends = jnp.stack([a[local_len - (KW - 1) :] for a in (query_in, key_in, value_in)])
     border = lax.ppermute(ends, "seq", [(i, i + 1) for i in range(parts - 1)])
@@ -180,19 +230,22 @@
     ).astype(jnp.bfloat16)
     mixed = lax.optimization_barrier(mixed.T)
 
-    outs = []
+    def slab_sum(weights):
+        terms = jnp.dot(mixed, weights, preferred_element_type=jnp.float32).astype(jnp.bfloat16)
+        if slabs != 2:
+            return [lax.psum_scatter(terms, "chan", scatter_dimension=1, tiled=True)]
+        own = terms.shape[1] // 2
+        sent = lax.dynamic_slice_in_dim(terms, (1 - chan) * own, own, 1)
+        kept = lax.dynamic_slice_in_dim(terms, chan * own, own, 1)
+        return [kept, lax.ppermute(sent, "chan", [(0, 1), (1, 0)])]
+
+    pairs = [(i, i ^ 1) for i in range(parts)]
+    pieces = []
     for weights in gathered:
-        terms = jnp.dot(mixed, weights, preferred_element_type=jnp.float32).astype(jnp.bfloat16)
-        if slabs == 2:
-            own = terms.shape[1] // 2
-            sent = lax.dynamic_slice_in_dim(terms, (1 - chan) * own, own, 1)
-            kept = lax.dynamic_slice_in_dim(terms, chan * own, own, 1)
-            got = lax.ppermute(sent, "chan", [(0, 1), (1, 0)])
-            summed = (kept.astype(jnp.float32) + got.astype(jnp.float32)).astype(jnp.bfloat16)
-        else:
-            summed = lax.psum_scatter(terms, "chan", scatter_dimension=1, tiled=True)
-        outs.append(summed.reshape(local_len, -1, chunk))
-    return jnp.stack(outs, axis=2).reshape(local_len, -1)
+        others = lax.ppermute(weights, "seq", pairs)
+        pieces.append([slab_sum(weights), slab_sum(others)])
+    core = (lax.axis_index("seq") % 2).astype(jnp.int32).reshape(1)
+    return join(core, pieces, local_len, chunk)
 
 
 def solution(mesh):

time: 462 us -> 501 us (1.084)
  waiting for transfers between devices: 212 us -> 324 us
  Pallas kernels: 109 us -> 57.7 us
  local copies, waits for them, and re-layouts: 34.8 us -> 23 us
  other arithmetic: 12.8 us -> 4.11 us
  matrix products: 33.3 us -> 28 us
    all_gather x4, waiting for transfers between devices: 64.2 us -> 208 us  [on_device(): lax.all_gather(w_out[:, at:at + chunk], 'seq', axis=1, tiled=True, axis_i...]
    all_to_all x1, waiting for transfers between devices: 65.5 us -> 0.01 us  [on_device(): conv = lax.all_to_all(conv, 'seq', split_axis=0, concat_axis=0, tiled=True)]
    pallas_call x1, Pallas kernels: 101 us -> 45.2 us  [long_conv(): pl.pallas_call(functools.partial(conv_kernel, parts, blocks), grid=(group...]
    ppermute x4 -> x12, waiting for transfers between devices: 17.9 us -> 51.5 us  [the longest x8 51.5 us: slab_sum(): return [kept, lax.ppermute(sent, 'chan', [(0, 1), (1, 0)])]]
    reshape x1 -> x0, local copies, waits for them, and re-layouts: 7.78 us -> none  [on_device(): return jnp.stack(outs, axis=2).reshape(local_len, -1)]
    another operation x1 -> x0, local copies, waits for them, and re-layouts: 7.37 us -> none  [on_device(): return jnp.stack(outs, axis=2).reshape(local_len, -1)]
    unnamed x4 -> x0, other arithmetic: 6.93 us -> none
    dot_general x4 -> x8, matrix products: 33.3 us -> 28 us  [slab_sum(): jnp.dot(mixed, weights, preferred_element_type=jnp.float32)]
  transfers between devices with their start and end apart: 12 -> 20, of which waited for: 4 -> 9; matrix products, arithmetic and copies ran while one was open for 11% -> 8% of each run, Pallas kernels for 24% -> 11%
where the time goes in v2:
time: 501 us; the launch traced here: 500 us
  waiting for transfers between devices  324 us (65%)
  Pallas kernels  57.7 us (12%)
  starting transfers between devices  49 us (10%)
  matrix products  28 us (6%)
  local copies, waits for them, and re-layouts  23 us (5%)
  between operations  13.5 us (3%)
    all_gather x4, waiting for transfers between devices, on_device(): lax.all_gather(w_out[:, at:at + chunk], 'seq', axis=1, tiled=True, axis_i...  208 us
    all_to_all x1, waiting for transfers between devices, on_device(): lax.all_to_all(gated.reshape(parts, -1, local_len), 'seq', split_axis=0,...  62.8 us
    ppermute x8, waiting for transfers between devices, slab_sum(): return [kept, lax.ppermute(sent, 'chan', [(0, 1), (1, 0)])]  51.5 us
    pallas_call x1, Pallas kernels, long_conv(): pl.pallas_call(functools.partial(conv_kernel, parts, blocks), grid=(group...  45.2 us
    dot_general x8, matrix products, slab_sum(): jnp.dot(mixed, weights, preferred_element_type=jnp.float32)  28 us
    all_to_all x1, starting transfers between devices, on_device(): conv = lax.all_to_all(conv, 'seq', split_axis=0, concat_axis=0, tiled=True)  24.7 us
    unnamed x42, local copies, waits for them, and re-layouts  13.6 us
  transfers between devices with their start and end apart: 20, of which 9 were waited for; matrix products, arithmetic and copies ran while one was open for 8% of the time, Pallas kernels for 11%

profile of v2, /device:TPU:0, one launch (start us, length us, event | category | flops | bytes accessed | tf_op | source)
XLA Modules:
  0.0 499.6 jit_solution(2820755188189365734)
XLA Ops:
  6.5 3.1 fusion.3
  12.1 2.4 collective-permute-start
  15.1 7.2 %all-to-all-start.1 = ((bf16[16,8,512]{2,1,0:T(8,128)(2,1)}), bf16[16,8,512]{2,1,0:T(8,128)(2,1)S(1)}, u32[]{:S(2)}, u32[]{:S(2)}) async-start(bf16[16,8,512]{2,1,0:T(8,128)(2,1)} %convert_bitcast_fusion.1), calls=%async_computation.1 | async-start | bytes 262144 | tf_op jit(solution)/shard_map/all_to_all | solution.py:205
  25.6 7.4 %shard_map.73 = (bf16[2048,512]{1,0:T(8,128)(2,1)S(1)}, bf16[2048,512]{1,0:T(8,128)(2,1)}) custom-call(bf16[512,2048]{1,0:T(8,128)(2,1)S(1)} %copy-done, bf16[512,2048]{1,0:T(8,128)(2,1)S(1)} %copy-done.1, bf16[512,2048]{1,0:T(8,128)(2,1)S(1)} %copy-done.2, f32[3,8,2048]{2,1,0:T(8,128)S(1)} %pad_convert_fusion.border_ref, f32[3,3,2048]{2,1,0:T(4,128)S(1)} %copy-done.14), custom_call_target="tpu_custom_call" | custom-call | flops 20971520 | bytes 10485760 | tf_op jit(solution)/shard_map/pallas_call | solution.py:40
  34.3 6.0 %all-to-all-start = ((bf16[16,128,512]{2,1,0:T(8,128)(2,1)}), bf16[16,128,512]{2,1,0:T(8,128)(2,1)S(1)}, u32[]{:S(2)}, u32[]{:S(2)}) async-start(bf16[16,128,512]{2,1,0:T(8,128)(2,1)} %bitcast.4), calls=%async_computation | async-start | bytes 4194304 | tf_op jit(solution)/shard_map/all_to_all | solution.py:221
  41.2 62.8 %all-to-all-done.data_ref = bf16[16,128,512]{2,1,0:T(8,128)(2,1)S(1)} async-done(((bf16[16,128,512]{2,1,0:T(8,128)(2,1)}), bf16[16,128,512]{2,1,0:T(8,128)(2,1)S(1)}, u32[]{:S(2)}, u32[]{:S(2)}) %all-to-all-start) | async-done | bytes 2097184 | tf_op jit(solution)/shard_map/all_to_all | solution.py:221
  104.0 45.2 %shard_map.74 = bf16[16,128,512]{2,1,0:T(8,128)(2,1)S(1)} custom-call(bf16[16,128,512]{2,1,0:T(8,128)(2,1)S(1)} %all-to-all-done.data_ref, f32[8,8,1152]{2,1,0:T(8,128)S(1)} %select_maximum_fusion.lags_ref), custom_call_target="tpu_custom_call" | custom-call | flops 17179869184 | bytes 4194304 | tf_op jit(solution)/shard_map/pallas_call | solution.py:128
  150.5 24.7 %all-to-all-start.2 = ((bf16[16,128,512]{2,1,0:T(8,128)(2,1)}), bf16[16,128,512]{2,1,0:T(8,128)(2,1)}, u32[]{:S(2)}, u32[]{:S(2)}) async-start(bf16[16,128,512]{2,1,0:T(8,128)(2,1)} %copy-done.5), calls=%async_computation.2 | async-start | bytes 4194304 | tf_op jit(solution)/shard_map/all_to_all | solution.py:225
  175.5 57.8 %all-gather.7.cloned.1.call-done = bf16[2048,1024]{1,0:T(8,128)(2,1)} async-done(((bf16[2048,128]{1,0:T(8,128)(2,1)}), bf16[2048,1024]{1,0:T(8,128)(2,1)}) %all-gather.7.cloned.1.call-update) | async-done | bytes 4194320 | tf_op jit(solution)/shard_map/all_gather | solution.py:199
  233.4 75.1 %all-gather.9.cloned.1.call-done = bf16[2048,1024]{1,0:T(8,128)(2,1)} async-done(((bf16[2048,128]{1,0:T(8,128)(2,1)}), bf16[2048,1024]{1,0:T(8,128)(2,1)}) %all-gather.9.cloned.1.call-update) | async-done | bytes 4194320 | tf_op jit(solution)/shard_map/all_gather | solution.py:199
  308.5 75.1 %all-gather.11.cloned.1.call-done = bf16[2048,1024]{1,0:T(8,128)(2,1)} async-done(((bf16[2048,128]{1,0:T(8,128)(2,1)}), bf16[2048,1024]{1,0:T(8,128)(2,1)}) %all-gather.11.cloned.1.call-update) | async-done | bytes 4194320 | tf_op jit(solution)/shard_map/all_gather | solution.py:199
  383.7 3.3 fusion.2
  391.2 2.4 convolution_convert_fusion.5
  396.2 2.4 convolution_convert_fusion.1
  400.0 4.6 convolution_convert_fusion.6
  407.0 4.6 convolution_convert_fusion.4
  412.2 4.8 convolution_convert_fusion.2
  418.6 4.6 convolution_convert_fusion
  431.3 6.9 %collective-permute-done.10.refs_13_ = bf16[512,512]{1,0:T(8,128)(2,1)} collective-permute-done((bf16[512,512]{1,0:T(8,128)(2,1)}, bf16[512,512]{1,0:T(8,128)(2,1)}, u32[]{:S(2)}, u32[]{:S(2)}) %collective-permute-start.10) | collective-permute-done | bytes 524320 | tf_op jit(solution)/shard_map/ppermute | solution.py:240
  438.2 11.2 %collective-permute-done.3.refs_3_ = bf16[512,512]{1,0:T(8,128)(2,1)} collective-permute-done((bf16[512,512]{1,0:T(8,128)(2,1)}, bf16[512,512]{1,0:T(8,128)(2,1)}, u32[]{:S(2)}, u32[]{:S(2)}) %collective-permute-start.3) | collective-permute-done | bytes 524320 | tf_op jit(solution)/shard_map/ppermute | solution.py:240
  449.4 11.2 %collective-permute-done.6.refs_7_ = bf16[512,512]{1,0:T(8,128)(2,1)} collective-permute-done((bf16[512,512]{1,0:T(8,128)(2,1)}, bf16[512,512]{1,0:T(8,128)(2,1)}, u32[]{:S(2)}, u32[]{:S(2)}) %collective-permute-start.6) | collective-permute-done | bytes 524320 | tf_op jit(solution)/shard_map/ppermute | solution.py:240
  460.7 11.2 %collective-permute-done.9.refs_11_ = bf16[512,512]{1,0:T(8,128)(2,1)} collective-permute-done((bf16[512,512]{1,0:T(8,128)(2,1)}, bf16[512,512]{1,0:T(8,128)(2,1)}, u32[]{:S(2)}, u32[]{:S(2)}) %collective-permute-start.9) | collective-permute-done | bytes 524320 | tf_op jit(solution)/shard_map/ppermute | solution.py:240
  471.9 10.8 %collective-permute-done.12.refs_15_ = bf16[512,512]{1,0:T(8,128)(2,1)} collective-permute-done((bf16[512,512]{1,0:T(8,128)(2,1)}, bf16[512,512]{1,0:T(8,128)(2,1)}, u32[]{:S(2)}, u32[]{:S(2)}) %collective-permute-start.12) | collective-permute-done | bytes 524320 | tf_op jit(solution)/shard_map/ppermute | solution.py:240
  488.0 5.1 %shard_map.75 = bf16[512,4096]{1,0:T(8,128)(2,1)} custom-call(s32[1]{0:T(128)} %bitcast.core_ref, bf16[512,512]{1,0:T(8,128)(2,1)S(1)} %get-tuple-element.28.refs_0_, bf16[512,512]{1,0:T(8,128)(2,1)S(1)} %copy-done.9, bf16[512,512]{1,0:T(8,128)(2,1)S(1)} %get-tuple-element.26.refs_2_, bf16[512,512]{1,0:T(8,128)(2,1)} %collective-permute-done.3.refs_3_, ...), custom_call_target="tpu_custom_call" | custom-call | tf_op jit(solution)/shard_map/pallas_call | solution.py:179
  (93 shorter events, 36.0 us)
Async XLA Ops:
  6.5 7.9 %copy-start.15 = (f32[128,512]{1,0:T(8,128)S(1)}, f32[128,512]{1,0:T(8,128)}, u32[]{:S(2)}) copy-start(f32[128,512]{1,0:T(8,128)} %param.11) | copy-start | bytes 786436
  6.5 168.7 %all-gather.5.cloned.1.call-start = ((), (), s32[]{:S(2)}) async-start(), calls=%async_computation.3 | async-start | bytes 4718592 | tf_op jit(solution)/shard_map/all_gather | solution.py:199
  9.7 12.7 %copy-start.14 = (f32[3,3,2048]{2,1,0:T(4,128)S(1)}, f32[3,3,2048]{2,1,0:T(4,128)}, u32[]{:S(2)}) copy-start(f32[3,3,2048]{2,1,0:T(4,128)} %taps_ref.1) | copy-start | bytes 221188
  9.7 223.7 %all-gather.7.cloned.1.call-start = ((), (), s32[]{:S(2)}) async-start(), calls=%async_computation.4 | async-start | bytes 4718592 | tf_op jit(solution)/shard_map/all_gather | solution.py:199
  10.4 298.1 %all-gather.9.cloned.1.call-start = ((), (), s32[]{:S(2)}) async-start(), calls=%async_computation.5 | async-start | bytes 4718592 | tf_op jit(solution)/shard_map/all_gather | solution.py:199
  12.1 10.2 %collective-permute-start = (bf16[3,2,2048]{2,1,0:T(2,128)(2,1)S(1)}, bf16[3,2,2048]{2,1,0:T(2,128)(2,1)S(1)}, u32[]{:S(2)}, u32[]{:S(2)}) collective-permute-start(bf16[3,2,2048]{2,1,0:T(2,128)(2,1)S(1)} %pad_maximum_fusion), channel_id=1, source_target_pairs={{0,2},{2,4},{4,6},{6,8},{8,10},{10,12},{12,14},{14,16},{16,18},{18... | collective-permute-start | bytes 73736 | tf_op jit(solution)/shard_map/ppermute | solution.py:218
  15.1 19.1 %all-to-all-start.1 = ((bf16[16,8,512]{2,1,0:T(8,128)(2,1)}), bf16[16,8,512]{2,1,0:T(8,128)(2,1)S(1)}, u32[]{:S(2)}, u32[]{:S(2)}) async-start(bf16[16,8,512]{2,1,0:T(8,128)(2,1)} %convert_bitcast_fusion.1), calls=%async_computation.1 | async-start | bytes 262144 | tf_op jit(solution)/shard_map/all_to_all | solution.py:205
  34.3 69.7 %all-to-all-start = ((bf16[16,128,512]{2,1,0:T(8,128)(2,1)}), bf16[16,128,512]{2,1,0:T(8,128)(2,1)S(1)}, u32[]{:S(2)}, u32[]{:S(2)}) async-start(bf16[16,128,512]{2,1,0:T(8,128)(2,1)} %bitcast.4), calls=%async_computation | async-start | bytes 4194304 | tf_op jit(solution)/shard_map/all_to_all | solution.py:221
  40.3 343.4 %all-gather.11.cloned.1.call-start = ((), (), s32[]{:S(2)}) async-start(), calls=%async_computation.6 | async-start | bytes 4718592 | tf_op jit(solution)/shard_map/all_gather | solution.py:199
  150.5 233.2 %copy-start.4 = (bf16[2048,512]{1,0:T(8,128)(2,1)S(1)}, bf16[2048,512]{1,0:T(8,128)(2,1)}, u32[]{:S(2)}) copy-start(bf16[2048,512]{1,0:T(8,128)(2,1)} %copy-done.3) | copy-start | bytes 6291460
  150.5 233.2 %copy-start.16 = (f32[2048]{0:T(1024)S(1)}, f32[2048]{0:T(1024)}, u32[]{:S(2)}) copy-start(f32[2048]{0:T(1024)} %param.12) | copy-start | bytes 24580
  150.5 233.1 %all-to-all-start.2 = ((bf16[16,128,512]{2,1,0:T(8,128)(2,1)}), bf16[16,128,512]{2,1,0:T(8,128)(2,1)}, u32[]{:S(2)}, u32[]{:S(2)}) async-start(bf16[16,128,512]{2,1,0:T(8,128)(2,1)} %copy-done.5), calls=%async_computation.2 | async-start | bytes 4194304 | tf_op jit(solution)/shard_map/all_to_all | solution.py:225
  175.3 224.2 %collective-permute-start.2 = (bf16[2048,1024]{1,0:T(8,128)(2,1)}, bf16[2048,1024]{1,0:T(8,128)(2,1)}, u32[]{:S(2)}, u32[]{:S(2)}) collective-permute-start(bf16[2048,1024]{1,0:T(8,128)(2,1)} %all-gather.5.cloned.1.call-done), channel_id=1, source_target_pairs={{0,2},{2,0},{4,6},{6,4},{8,10},{10,8},{12,14},{14,12},{16,18},{18,... | collective-permute-start | bytes 12582920 | tf_op jit(solution)/shard_map/ppermute | solution.py:245
  233.4 172.2 %collective-permute-start.5 = (bf16[2048,1024]{1,0:T(8,128)(2,1)}, bf16[2048,1024]{1,0:T(8,128)(2,1)}, u32[]{:S(2)}, u32[]{:S(2)}) collective-permute-start(bf16[2048,1024]{1,0:T(8,128)(2,1)} %all-gather.7.cloned.1.call-done), channel_id=1, source_target_pairs={{0,2},{2,0},{4,6},{6,4},{8,10},{10,8},{12,14},{14,12},{16,18},{18,... | collective-permute-start | bytes 12582920 | tf_op jit(solution)/shard_map/ppermute | solution.py:245
  308.5 103.1 %collective-permute-start.8 = (bf16[2048,1024]{1,0:T(8,128)(2,1)}, bf16[2048,1024]{1,0:T(8,128)(2,1)}, u32[]{:S(2)}, u32[]{:S(2)}) collective-permute-start(bf16[2048,1024]{1,0:T(8,128)(2,1)} %all-gather.9.cloned.1.call-done), channel_id=1, source_target_pairs={{0,2},{2,0},{4,6},{6,4},{8,10},{10,8},{12,14},{14,12},{16,18},{18,... | collective-permute-start | bytes 12582920 | tf_op jit(solution)/shard_map/ppermute | solution.py:245
  383.7 33.4 %collective-permute-start.11 = (bf16[2048,1024]{1,0:T(8,128)(2,1)}, bf16[2048,1024]{1,0:T(8,128)(2,1)}, u32[]{:S(2)}, u32[]{:S(2)}) collective-permute-start(bf16[2048,1024]{1,0:T(8,128)(2,1)} %all-gather.11.cloned.1.call-done), channel_id=1, source_target_pairs={{0,2},{2,0},{4,6},{6,4},{8,10},{10,8},{12,14},{14,12},{16,18},{18,... | collective-permute-start | bytes 12582920 | tf_op jit(solution)/shard_map/ppermute | solution.py:245
  389.6 36.7 %collective-permute-start.1 = (bf16[512,512]{1,0:T(8,128)(2,1)S(1)}, bf16[512,512]{1,0:T(8,128)(2,1)S(1)}, u32[]{:S(2)}, u32[]{:S(2)}) collective-permute-start(bf16[512,512]{1,0:T(8,128)(2,1)S(1)} %get-tuple-element.27), channel_id=1, source_target_pairs={{0,1},{1,0},{2,3},{3,2},{4,5},{5,4},{6,7},{7,6},{8,9},{9,8},{10,11... | collective-permute-start | bytes 1572872 | tf_op jit(solution)/shard_map/ppermute | solution.py:240
  399.5 28.1 %collective-permute-start.4 = (bf16[512,512]{1,0:T(8,128)(2,1)S(1)}, bf16[512,512]{1,0:T(8,128)(2,1)S(1)}, u32[]{:S(2)}, u32[]{:S(2)}) collective-permute-start(bf16[512,512]{1,0:T(8,128)(2,1)S(1)} %get-tuple-element.23), channel_id=1, source_target_pairs={{0,1},{1,0},{2,3},{3,2},{4,5},{5,4},{6,7},{7,6},{8,9},{9,8},{10,11... | collective-permute-start | bytes 1572872 | tf_op jit(solution)/shard_map/ppermute | solution.py:240
  405.6 24.4 %collective-permute-start.7 = (bf16[512,512]{1,0:T(8,128)(2,1)S(1)}, bf16[512,512]{1,0:T(8,128)(2,1)S(1)}, u32[]{:S(2)}, u32[]{:S(2)}) collective-permute-start(bf16[512,512]{1,0:T(8,128)(2,1)S(1)} %get-tuple-element.19), channel_id=1, source_target_pairs={{0,1},{1,0},{2,3},{3,2},{4,5},{5,4},{6,7},{7,6},{8,9},{9,8},{10,11... | collective-permute-start | bytes 1572872 | tf_op jit(solution)/shard_map/ppermute | solution.py:240
  411.6 26.6 %collective-permute-start.10 = (bf16[512,512]{1,0:T(8,128)(2,1)}, bf16[512,512]{1,0:T(8,128)(2,1)}, u32[]{:S(2)}, u32[]{:S(2)}) collective-permute-start(bf16[512,512]{1,0:T(8,128)(2,1)} %get-tuple-element.15), channel_id=1, source_target_pairs={{0,1},{1,0},{2,3},{3,2},{4,5},{5,4},{6,7},{7,6},{8,9},{9,8},{10,11... | collective-permute-start | bytes 1572872 | tf_op jit(solution)/shard_map/ppermute | solution.py:240
  417.1 32.4 %collective-permute-start.3 = (bf16[512,512]{1,0:T(8,128)(2,1)}, bf16[512,512]{1,0:T(8,128)(2,1)}, u32[]{:S(2)}, u32[]{:S(2)}) collective-permute-start(bf16[512,512]{1,0:T(8,128)(2,1)} %get-tuple-element.25), channel_id=1, source_target_pairs={{0,1},{1,0},{2,3},{3,2},{4,5},{5,4},{6,7},{7,6},{8,9},{9,8},{10,11... | collective-permute-start | bytes 1572872 | tf_op jit(solution)/shard_map/ppermute | solution.py:240
  427.1 33.6 %collective-permute-start.6 = (bf16[512,512]{1,0:T(8,128)(2,1)}, bf16[512,512]{1,0:T(8,128)(2,1)}, u32[]{:S(2)}, u32[]{:S(2)}) collective-permute-start(bf16[512,512]{1,0:T(8,128)(2,1)} %get-tuple-element.21), channel_id=1, source_target_pairs={{0,1},{1,0},{2,3},{3,2},{4,5},{5,4},{6,7},{7,6},{8,9},{9,8},{10,11... | collective-permute-start | bytes 1572872 | tf_op jit(solution)/shard_map/ppermute | solution.py:240
  428.5 43.5 %collective-permute-start.9 = (bf16[512,512]{1,0:T(8,128)(2,1)}, bf16[512,512]{1,0:T(8,128)(2,1)}, u32[]{:S(2)}, u32[]{:S(2)}) collective-permute-start(bf16[512,512]{1,0:T(8,128)(2,1)} %get-tuple-element.17), channel_id=1, source_target_pairs={{0,1},{1,0},{2,3},{3,2},{4,5},{5,4},{6,7},{7,6},{8,9},{9,8},{10,11... | collective-permute-start | bytes 1572872 | tf_op jit(solution)/shard_map/ppermute | solution.py:240
  430.7 52.0 %collective-permute-start.12 = (bf16[512,512]{1,0:T(8,128)(2,1)}, bf16[512,512]{1,0:T(8,128)(2,1)}, u32[]{:S(2)}, u32[]{:S(2)}) collective-permute-start(bf16[512,512]{1,0:T(8,128)(2,1)} %get-tuple-element.13), channel_id=1, source_target_pairs={{0,1},{1,0},{2,3},{3,2},{4,5},{5,4},{6,7},{7,6},{8,9},{9,8},{10,11... | collective-permute-start | bytes 1572872 | tf_op jit(solution)/shard_map/ppermute | solution.py:240
  (17 other events, 30.6 us)
Sparse Core Ops, SparseCore 0:
  9.8 115.2 all-gather.4
  127.2 106.1 all-gather.6
  235.4 73.0 all-gather.8
  310.4 73.1 all-gather.10

commit v3 on v2

--- a/solution.py
+++ b/solution.py
@@ -148,43 +148,33 @@
     )(data, lags)
 
 
-def join_kernel(shape, chunk, core_ref, *refs):
-    chunks, addends, pairs = shape
+def join_kernel(shape, chunk, *refs):
+    chunks, addends, owners = shape
     out_ref = refs[-1]
-
-    def place(core):
-        for at in range(chunks):
-            for side in range(2):
-                first = (at * 2 + side) * addends
-                for pair in range(pairs):
-                    cols = slice(pair * chunk, (pair + 1) * chunk)
-                    total = refs[first][:, cols]
-                    if addends == 2:
-                        more = refs[first + 1][:, cols].astype(jnp.float32)
-                        total = (total.astype(jnp.float32) + more).astype(jnp.bfloat16)
-                    owner = pair * 2 + (core + side) % 2
-                    to = (owner * chunks + at) * chunk
-                    out_ref[:, to : to + chunk] = total
-
-    for core in range(2):
-        pl.when(core_ref[0] == core)(functools.partial(place, core))
-
-
-def join(core, pieces, local_len, chunk):
-    flat = [array for both in pieces for side in both for array in side]
-    addends = len(pieces[0][0])
+    for at in range(chunks):
+        for owner in range(owners):
+            cols = slice(owner * chunk, (owner + 1) * chunk)
+            total = refs[at * addends][:, cols]
+            if addends == 2:
+                more = refs[at * addends + 1][:, cols].astype(jnp.float32)
+                total = (total.astype(jnp.float32) + more).astype(jnp.bfloat16)
+            to = (owner * chunks + at) * chunk
+            out_ref[:, to : to + chunk] = total
+
+
+def join(pieces, local_len, chunk):
+    flat = [array for piece in pieces for array in piece]
     wide = flat[0].shape[1]
     rows = 128
-    total = 2 * len(pieces) * wide
+    total = len(pieces) * wide
     return pl.pallas_call(
-        functools.partial(join_kernel, (len(pieces), addends, wide // chunk), chunk),
+        functools.partial(join_kernel, (len(pieces), len(pieces[0]), wide // chunk), chunk),
         grid=(local_len // rows,),
-        in_specs=[pl.BlockSpec(memory_space=pltpu.SMEM)]
-        + [pl.BlockSpec((rows, wide), lambda i: (i, 0))] * len(flat),
+        in_specs=[pl.BlockSpec((rows, wide), lambda i: (i, 0))] * len(flat),
         out_specs=pl.BlockSpec((rows, total), lambda i: (i, 0)),
         out_shape=jax.ShapeDtypeStruct((local_len, total), jnp.bfloat16),
         compiler_params=pltpu.CompilerParams(vmem_limit_bytes=32 * 1024 * 1024),
-    )(core, *flat)
+    )(*flat)
 
 
 def on_device(query_in, key_in, value_in, short_weight, long_filter, skip_gain, w_out):
@@ -194,11 +184,8 @@
     chan = lax.axis_index("chan")
     columns = w_out.shape[1]
     chunk = 128
-    same_core = [list(range(core, parts, 2)) for core in range(2)]
     gathered = [
-        lax.all_gather(
-            w_out[:, at : at + chunk], "seq", axis=1, tiled=True, axis_index_groups=same_core
-        )
+        lax.all_gather(w_out[:, at : at + chunk], "seq", axis=1, tiled=True)
         for at in range(0, columns, chunk)
     ]
 
@@ -239,13 +226,7 @@
         kept = lax.dynamic_slice_in_dim(terms, chan * own, own, 1)
         return [kept, lax.ppermute(sent, "chan", [(0, 1), (1, 0)])]
 
-    pairs = [(i, i ^ 1) for i in range(parts)]
-    pieces = []
-    for weights in gathered:
-        others = lax.ppermute(weights, "seq", pairs)
-        pieces.append([slab_sum(weights), slab_sum(others)])
-    core = (lax.axis_index("seq") % 2).astype(jnp.int32).reshape(1)
-    return join(core, pieces, local_len, chunk)
+    return join([slab_sum(weights) for weights in gathered], local_len, chunk)
 
 
 def solution(mesh):

time: 501 us -> 443 us (0.88)
  waiting for transfers between devices: 324 us -> 273 us
  local copies, waits for them, and re-layouts: 23 us -> 13.6 us
  matrix products: 28 us -> 34 us
    all_gather x4, waiting for transfers between devices: 208 us -> 121 us  [on_device(): lax.all_gather(w_out[:, at:at + chunk], 'seq', axis=1, tiled=True)]
    all_to_all x1, waiting for transfers between devices: 0.01 us -> 63.7 us  [on_device(): conv = lax.all_to_all(conv, 'seq', split_axis=0, concat_axis=0, tiled=True)]
    ppermute x8 -> x4, waiting for transfers between devices: 51.5 us -> 23.8 us  [slab_sum(): return [kept, lax.ppermute(sent, 'chan', [(0, 1), (1, 0)])]]
    unnamed x42 -> x20, local copies, waits for them, and re-layouts: 13.6 us -> 5.82 us
    dot_general x8 -> x4, matrix products: 28 us -> 34 us  [slab_sum(): jnp.dot(mixed, weights, preferred_element_type=jnp.float32)]
  transfers between devices with their start and end apart: 20 -> 12, of which waited for: 9 -> 5; matrix products, arithmetic and copies ran while one was open for 8% -> 10% of each run, Pallas kernels for 11% -> 12%
where the time goes in v3:
time: 443 us
  waiting for transfers between devices  273 us (62%)
  Pallas kernels  57.5 us (13%)
  starting transfers between devices  45.4 us (10%)
  matrix products  34 us (8%)
  local copies, waits for them, and re-layouts  13.6 us (3%)
  between operations  13.3 us (3%)
  other arithmetic  5.28 us (1%)
    all_gather x4, waiting for transfers between devices, on_device(): lax.all_gather(w_out[:, at:at + chunk], 'seq', axis=1, tiled=True)  121 us
    all_to_all x1, waiting for transfers between devices, on_device(): conv = lax.all_to_all(conv, 'seq', split_axis=0, concat_axis=0, tiled=True)  63.7 us
    all_to_all x1, waiting for transfers between devices, on_device(): lax.all_to_all(gated.reshape(parts, -1, local_len), 'seq', split_axis=0,...  62.7 us
    pallas_call x1, Pallas kernels, long_conv(): pl.pallas_call(functools.partial(conv_kernel, parts, blocks), grid=(group...  45.3 us
    dot_general x4, matrix products, slab_sum(): jnp.dot(mixed, weights, preferred_element_type=jnp.float32)  34 us
    all_to_all x1, starting transfers between devices, on_device(): conv = lax.all_to_all(conv, 'seq', split_axis=0, concat_axis=0, tiled=True)  24.5 us
    ppermute x4, waiting for transfers between devices, slab_sum(): return [kept, lax.ppermute(sent, 'chan', [(0, 1), (1, 0)])]  23.8 us
  transfers between devices with their start and end apart: 12, of which 5 were waited for; matrix products, arithmetic and copies ran while one was open for 10% of the time, Pallas kernels for 12%

profile of v3, /device:TPU:0, one launch (start us, length us, event | category | flops | bytes accessed | tf_op | source)
XLA Modules:
  0.0 442.6 jit_solution(13078078218479185407)
XLA Ops:
  6.5 2.9 fusion.3
  12.5 2.4 collective-permute-start
  15.5 7.2 %all-to-all-start.1 = ((bf16[16,8,512]{2,1,0:T(8,128)(2,1)}), bf16[16,8,512]{2,1,0:T(8,128)(2,1)S(1)}, u32[]{:S(2)}, u32[]{:S(2)}) async-start(bf16[16,8,512]{2,1,0:T(8,128)(2,1)} %convert_bitcast_fusion.1), calls=%async_computation.1 | async-start | bytes 262144 | tf_op jit(solution)/shard_map/all_to_all | solution.py:192
  22.8 1.6 copy-done.1
  24.4 1.6 copy-done.2
  25.9 7.4 %shard_map.73 = (bf16[2048,512]{1,0:T(8,128)(2,1)S(1)}, bf16[2048,512]{1,0:T(8,128)(2,1)}) custom-call(bf16[512,2048]{1,0:T(8,128)(2,1)S(1)} %copy-done, bf16[512,2048]{1,0:T(8,128)(2,1)S(1)} %copy-done.1, bf16[512,2048]{1,0:T(8,128)(2,1)S(1)} %copy-done.2, f32[3,8,2048]{2,1,0:T(8,128)S(1)} %pad_convert_fusion.border_ref, f32[3,3,2048]{2,1,0:T(4,128)S(1)} %copy-done.6), custom_call_target="tpu_custom_call" | custom-call | flops 20971520 | bytes 10485760 | tf_op jit(solution)/shard_map/pallas_call | solution.py:40
  33.3 1.3 copy-done.3
  34.7 6.0 %all-to-all-start = ((bf16[16,128,512]{2,1,0:T(8,128)(2,1)}), bf16[16,128,512]{2,1,0:T(8,128)(2,1)S(1)}, u32[]{:S(2)}, u32[]{:S(2)}) async-start(bf16[16,128,512]{2,1,0:T(8,128)(2,1)} %bitcast.3), calls=%async_computation | async-start | bytes 4194304 | tf_op jit(solution)/shard_map/all_to_all | solution.py:208
  41.0 62.7 %all-to-all-done.data_ref = bf16[16,128,512]{2,1,0:T(8,128)(2,1)S(1)} async-done(((bf16[16,128,512]{2,1,0:T(8,128)(2,1)}), bf16[16,128,512]{2,1,0:T(8,128)(2,1)S(1)}, u32[]{:S(2)}, u32[]{:S(2)}) %all-to-all-start) | async-done | bytes 2097184 | tf_op jit(solution)/shard_map/all_to_all | solution.py:208
  103.7 45.3 %shard_map.74 = bf16[16,128,512]{2,1,0:T(8,128)(2,1)S(1)} custom-call(bf16[16,128,512]{2,1,0:T(8,128)(2,1)S(1)} %all-to-all-done.data_ref, f32[8,8,1152]{2,1,0:T(8,128)S(1)} %select_maximum_fusion.lags_ref), custom_call_target="tpu_custom_call" | custom-call | flops 17179869184 | bytes 4194304 | tf_op jit(solution)/shard_map/pallas_call | solution.py:128
  150.3 24.5 %all-to-all-start.2 = ((bf16[16,128,512]{2,1,0:T(8,128)(2,1)}), bf16[16,128,512]{2,1,0:T(8,128)(2,1)}, u32[]{:S(2)}, u32[]{:S(2)}) async-start(bf16[16,128,512]{2,1,0:T(8,128)(2,1)} %copy-done.5), calls=%async_computation.2 | async-start | bytes 4194304 | tf_op jit(solution)/shard_map/all_to_all | solution.py:212
  174.8 63.7 %all-to-all-done.2 = bf16[16,128,512]{2,1,0:T(8,128)(2,1)} async-done(((bf16[16,128,512]{2,1,0:T(8,128)(2,1)}), bf16[16,128,512]{2,1,0:T(8,128)(2,1)}, u32[]{:S(2)}, u32[]{:S(2)}) %all-to-all-start.2) | async-done | bytes 2097184 | tf_op jit(solution)/shard_map/all_to_all | solution.py:212
  238.5 4.5 %fusion.2 = bf16[512,2048]{0,1:T(8,128)(2,1)} fusion(bf16[2048,512]{1,0:T(8,128)(2,1)} %get-tuple-element.8, bf16[2048,512]{1,0:T(8,128)(2,1)S(1)} %copy-done.4, bf16[16,128,512]{2,1,0:T(8,128)(2,1)} %all-to-all-done.2, f32[2048]{0:T(1024)S(1)} %copy-done.9), kind=kLoop, calls=%fused_computation.7 | loop fusion | flops 7340032 | bytes 8396800 | tf_op jit(solution)/shard_map/transpose | solution.py:218
  243.0 8.6 %convolution_convert_fusion.3 = bf16[512,2048]{1,0:T(8,128)(2,1)S(1)} fusion(bf16[512,2048]{0,1:T(8,128)(2,1)} %fusion.2, bf16[2048,2048]{1,0:T(8,128)(2,1)} %all-gather.5.cloned.1.call-done), kind=kOutput, calls=%fused_computation.6 | convolution fusion | flops 4296015872 | bytes 12582912 | tf_op jit(solution)/shard_map/dot_general | solution.py:221
  252.8 1.5 collective-permute-start.1
  254.3 8.3 %convolution_convert_fusion.2 = bf16[512,2048]{1,0:T(8,128)(2,1)S(1)} fusion(bf16[512,2048]{0,1:T(8,128)(2,1)S(1)} %copy-done.7, bf16[2048,2048]{1,0:T(8,128)(2,1)} %all-gather.7.cloned.1.call-done), kind=kOutput, calls=%fused_computation.5 | convolution fusion | flops 4296015872 | bytes 12582912 | tf_op jit(solution)/shard_map/dot_general | solution.py:221
  264.6 54.2 %all-gather.9.cloned.1.call-done = bf16[2048,2048]{1,0:T(8,128)(2,1)} async-done(((bf16[2048,128]{1,0:T(8,128)(2,1)}), bf16[2048,2048]{1,0:T(8,128)(2,1)}) %all-gather.9.cloned.1.call-update) | async-done | bytes 8388624 | tf_op jit(solution)/shard_map/all_gather | solution.py:188
  318.7 8.6 %convolution_convert_fusion.1 = bf16[512,2048]{1,0:T(8,128)(2,1)S(1)} fusion(bf16[512,2048]{0,1:T(8,128)(2,1)} %fusion.2, bf16[2048,2048]{1,0:T(8,128)(2,1)} %all-gather.9.cloned.1.call-done), kind=kOutput, calls=%fused_computation.4 | convolution fusion | flops 4296015872 | bytes 12582912 | tf_op jit(solution)/shard_map/dot_general | solution.py:221
  328.5 1.5 collective-permute-start.3
  330.0 67.1 %all-gather.11.cloned.1.call-done = bf16[2048,2048]{1,0:T(8,128)(2,1)} async-done(((bf16[2048,128]{1,0:T(8,128)(2,1)}), bf16[2048,2048]{1,0:T(8,128)(2,1)}) %all-gather.11.cloned.1.call-update) | async-done | bytes 8388624 | tf_op jit(solution)/shard_map/all_gather | solution.py:188
  397.0 8.6 %convolution_convert_fusion = bf16[512,2048]{1,0:T(8,128)(2,1)S(1)} fusion(bf16[512,2048]{0,1:T(8,128)(2,1)} %fusion.2, bf16[2048,2048]{1,0:T(8,128)(2,1)} %all-gather.11.cloned.1.call-done), kind=kOutput, calls=%fused_computation.3 | convolution fusion | flops 4296015872 | bytes 12582912 | tf_op jit(solution)/shard_map/dot_general | solution.py:221
  405.8 1.5 collective-permute-start.4
  407.4 23.8 %collective-permute-done.4.refs_7_ = bf16[512,1024]{1,0:T(8,128)(2,1)S(1)} collective-permute-done((bf16[512,1024]{1,0:T(8,128)(2,1)S(1)}, bf16[512,1024]{1,0:T(8,128)(2,1)S(1)}, u32[]{:S(2)}, u32[]{:S(2)}) %collective-permute-start.4) | collective-permute-done | bytes 1048608 | tf_op jit(solution)/shard_map/ppermute | solution.py:227
  431.2 4.8 %shard_map.75 = bf16[512,4096]{1,0:T(8,128)(2,1)} custom-call(bf16[512,1024]{1,0:T(8,128)(2,1)S(1)} %get-tuple-element.20.refs_0_, bf16[512,1024]{1,0:T(8,128)(2,1)} %collective-permute-done.1.refs_1_, bf16[512,1024]{1,0:T(8,128)(2,1)S(1)} %get-tuple-element.18.refs_2_, bf16[512,1024]{1,0:T(8,128)(2,1)} %collective-permute-done.2.refs_3_, ...), custom_call_target="tpu_custom_call" | custom-call | tf_op jit(solution)/shard_map/pallas_call | solution.py:170
  (47 shorter events, 9.7 us)
Async XLA Ops:
  6.5 236.5 %all-gather.5.cloned.1.call-start = ((), (), s32[]{:S(2)}) async-start(), calls=%async_computation.3 | async-start | bytes 8912896 | tf_op jit(solution)/shard_map/all_gather | solution.py:188
  6.5 8.3 %copy-start.8 = (f32[128,512]{1,0:T(8,128)S(1)}, f32[128,512]{1,0:T(8,128)}, u32[]{:S(2)}) copy-start(f32[128,512]{1,0:T(8,128)} %param.11) | copy-start | bytes 786436
  9.5 2.1 copy-start
  9.5 13.3 %copy-start.6 = (f32[3,3,2048]{2,1,0:T(4,128)S(1)}, f32[3,3,2048]{2,1,0:T(4,128)}, u32[]{:S(2)}) copy-start(f32[3,3,2048]{2,1,0:T(4,128)} %taps_ref.1) | copy-start | bytes 221188
  9.5 244.8 %all-gather.7.cloned.1.call-start = ((), (), s32[]{:S(2)}) async-start(), calls=%async_computation.4 | async-start | bytes 8912896 | tf_op jit(solution)/shard_map/all_gather | solution.py:188
  10.3 308.5 %all-gather.9.cloned.1.call-start = ((), (), s32[]{:S(2)}) async-start(), calls=%async_computation.5 | async-start | bytes 8912896 | tf_op jit(solution)/shard_map/all_gather | solution.py:188
  11.0 386.0 %all-gather.11.cloned.1.call-start = ((), (), s32[]{:S(2)}) async-start(), calls=%async_computation.6 | async-start | bytes 8912896 | tf_op jit(solution)/shard_map/all_gather | solution.py:188
  12.5 10.2 %collective-permute-start = (bf16[3,2,2048]{2,1,0:T(2,128)(2,1)S(1)}, bf16[3,2,2048]{2,1,0:T(2,128)(2,1)S(1)}, u32[]{:S(2)}, u32[]{:S(2)}) collective-permute-start(bf16[3,2,2048]{2,1,0:T(2,128)(2,1)S(1)} %pad_maximum_fusion), channel_id=1, source_target_pairs={{0,2},{2,4},{4,6},{6,8},{8,10},{10,12},{12,14},{14,16},{16,18},{18... | collective-permute-start | bytes 73736 | tf_op jit(solution)/shard_map/ppermute | solution.py:205
  15.5 19.1 %all-to-all-start.1 = ((bf16[16,8,512]{2,1,0:T(8,128)(2,1)}), bf16[16,8,512]{2,1,0:T(8,128)(2,1)S(1)}, u32[]{:S(2)}, u32[]{:S(2)}) async-start(bf16[16,8,512]{2,1,0:T(8,128)(2,1)} %convert_bitcast_fusion.1), calls=%async_computation.1 | async-start | bytes 262144 | tf_op jit(solution)/shard_map/all_to_all | solution.py:192
  22.8 1.6 copy-start.1
  24.4 1.6 copy-start.2
  33.3 1.3 copy-start.3
  34.7 69.0 %all-to-all-start = ((bf16[16,128,512]{2,1,0:T(8,128)(2,1)}), bf16[16,128,512]{2,1,0:T(8,128)(2,1)S(1)}, u32[]{:S(2)}, u32[]{:S(2)}) async-start(bf16[16,128,512]{2,1,0:T(8,128)(2,1)} %bitcast.3), calls=%async_computation | async-start | bytes 4194304 | tf_op jit(solution)/shard_map/all_to_all | solution.py:208
  149.0 1.3 copy-start.5
  150.3 88.2 %copy-start.4 = (bf16[2048,512]{1,0:T(8,128)(2,1)S(1)}, bf16[2048,512]{1,0:T(8,128)(2,1)}, u32[]{:S(2)}) copy-start(bf16[2048,512]{1,0:T(8,128)(2,1)} %copy-done.3) | copy-start | bytes 6291460
  150.3 88.2 %copy-start.9 = (f32[2048]{0:T(1024)S(1)}, f32[2048]{0:T(1024)}, u32[]{:S(2)}) copy-start(f32[2048]{0:T(1024)} %param.12) | copy-start | bytes 24580
  150.3 88.2 %all-to-all-start.2 = ((bf16[16,128,512]{2,1,0:T(8,128)(2,1)}), bf16[16,128,512]{2,1,0:T(8,128)(2,1)}, u32[]{:S(2)}, u32[]{:S(2)}) async-start(bf16[16,128,512]{2,1,0:T(8,128)(2,1)} %copy-done.5), calls=%async_computation.2 | async-start | bytes 4194304 | tf_op jit(solution)/shard_map/all_to_all | solution.py:212
  251.6 2.7 copy-start.7
  252.8 154.6 %collective-permute-start.1 = (bf16[512,1024]{1,0:T(8,128)(2,1)}, bf16[512,1024]{1,0:T(8,128)(2,1)}, u32[]{:S(2)}, u32[]{:S(2)}) collective-permute-start(bf16[512,1024]{1,0:T(8,128)(2,1)} %get-tuple-element.19), channel_id=1, source_target_pairs={{0,1},{1,0},{2,3},{3,2},{4,5},{5,4},{6,7},{7,6},{8,9},{9,8},{10,11... | collective-permute-start | bytes 3145736 | tf_op jit(solution)/shard_map/ppermute | solution.py:227
  263.8 143.6 %collective-permute-start.2 = (bf16[512,1024]{1,0:T(8,128)(2,1)}, bf16[512,1024]{1,0:T(8,128)(2,1)}, u32[]{:S(2)}, u32[]{:S(2)}) collective-permute-start(bf16[512,1024]{1,0:T(8,128)(2,1)} %get-tuple-element.17), channel_id=1, source_target_pairs={{0,1},{1,0},{2,3},{3,2},{4,5},{5,4},{6,7},{7,6},{8,9},{9,8},{10,11... | collective-permute-start | bytes 3145736 | tf_op jit(solution)/shard_map/ppermute | solution.py:227
  328.5 78.9 %collective-permute-start.3 = (bf16[512,1024]{1,0:T(8,128)(2,1)}, bf16[512,1024]{1,0:T(8,128)(2,1)}, u32[]{:S(2)}, u32[]{:S(2)}) collective-permute-start(bf16[512,1024]{1,0:T(8,128)(2,1)} %get-tuple-element.15), channel_id=1, source_target_pairs={{0,1},{1,0},{2,3},{3,2},{4,5},{5,4},{6,7},{7,6},{8,9},{9,8},{10,11... | collective-permute-start | bytes 3145736 | tf_op jit(solution)/shard_map/ppermute | solution.py:227
  405.8 25.4 %collective-permute-start.4 = (bf16[512,1024]{1,0:T(8,128)(2,1)S(1)}, bf16[512,1024]{1,0:T(8,128)(2,1)S(1)}, u32[]{:S(2)}, u32[]{:S(2)}) collective-permute-start(bf16[512,1024]{1,0:T(8,128)(2,1)S(1)} %get-tuple-element.9), channel_id=1, source_target_pairs={{0,1},{1,0},{2,3},{3,2},{4,5},{5,4},{6,7},{7,6},{8,9},{9,8},{10,11... | collective-permute-start | bytes 3145736 | tf_op jit(solution)/shard_map/ppermute | solution.py:227
Sparse Core Ops, SparseCore 0:
  9.6 118.2 all-gather.4
  130.1 109.1 all-gather.6
  241.4 77.2 all-gather.8
  320.7 76.2 all-gather.10
